TPU v7x, 512 devices: a whole 4x8x8 slice. The times are simulated.
512 devices in a mesh: ctx: 64 (over z_hi, y, core), kvh: 8 (over x, z_lo).
Axes of the slice: x: 4, y: 8, z: 8 (z_hi: 4, z_lo: 2; z = z_hi * 2 + z_lo), core: 2. Of those that a mesh axis runs over, the one named last changes fastest.
Arguments:
- queries: bfloat16 [24576, 64, 128], P(('ctx', 'kvh')), may hold values from -160 to 160
- keys: bfloat16 [24576, 8, 128], P(('ctx', 'kvh')), may hold values from -6 to 6
- values: bfloat16 [24576, 8, 128], P(('ctx', 'kvh')), may hold values from -6 to 6
- grad_out: bfloat16 [24576, 64, 128], P(('ctx', 'kvh')), may hold values from -6 to 6
- segment_ids: int32 [24576], replicated, may hold values from 0 to 63, never falling along the last dimension, each value on 1 to 1152 neighbouring positions
Outputs:
- attention: bfloat16 [24576, 64, 128], P('ctx', 'kvh')
- grad_queries: bfloat16 [24576, 64, 128], P('ctx', 'kvh')
- grad_keys: bfloat16 [24576, 8, 128], P('ctx', 'kvh')
- grad_values: bfloat16 [24576, 8, 128], P('ctx', 'kvh')
Inputs may be any that keep to these rules, and one draw needn't show every extreme that they name: `segment_ids`: Non-decreasing from 0 without gaps; every document has 1 to 1152 positions, and one has exactly that many.
All inputs are finite; a program needn't handle non-finite values.
Results may differ from a plain program's by a relative error of at most 0.013.
Values may be sent and summed in bfloat16 or wider, within the bound.
A program may use at most 64 MiB of HBM per device.

v0:
```python
import math

import jax
import jax.numpy as jnp
from jax import lax
from jax.sharding import PartitionSpec as P

SPAN = 3


def passed_along(value, axis, steps):
    count = lax.axis_size(axis)
    leading, last = (max(0, -steps), min(count, count - steps))
    return lax.ppermute(value, axis, [(source, source + steps) for source in range(leading, last)])


def tile_math(query_pair, grad_pair, key_rows, value_rows, allowed, score_scale):
    scores = (
        jnp.einsum("bhd,wd->hbw", query_pair, key_rows, preferred_element_type=jnp.float32)
        * score_scale
    )
    scores = jnp.where(allowed[None], scores, -1e30)
    highest = jnp.max(scores, axis=-1, keepdims=True)
    log_total = highest + jnp.log(jnp.sum(jnp.exp(scores - highest), axis=-1, keepdims=True))
    probs_full = jnp.exp(scores - log_total)
    probs_low = probs_full.astype(jnp.bfloat16)
    attended = jnp.einsum(
        "hbw,wd->bhd", probs_low, value_rows, preferred_element_type=jnp.float32
    ).astype(jnp.bfloat16)
    attended = lax.optimization_barrier(attended)
    grad_probs = jnp.einsum(
        "bhd,wd->hbw", grad_pair, value_rows, preferred_element_type=jnp.float32
    )
    deltas = jnp.sum(grad_pair.astype(jnp.float32) * attended.astype(jnp.float32), axis=-1).T[
        :, :, None
    ]
    grad_scores = (probs_full * (grad_probs - deltas) * score_scale).astype(jnp.bfloat16)
    grad_query = jnp.einsum(
        "hbw,wd->bhd", grad_scores, key_rows, preferred_element_type=jnp.float32
    ).astype(jnp.bfloat16)
    grad_key = jnp.einsum(
        "hbw,bhd->wd", grad_scores, query_pair, preferred_element_type=jnp.float32
    )
    grad_value = jnp.einsum("hbw,bhd->wd", probs_low, grad_pair, preferred_element_type=jnp.float32)
    return (attended, grad_query, grad_key, grad_value)


def window_mask(segment_ids, owner, block_rows, window_rows):
    row_start = owner * block_rows
    segments_padded = jnp.concatenate([jnp.full((SPAN * block_rows,), -1, jnp.int32), segment_ids])
    query_segments = lax.dynamic_slice_in_dim(segment_ids, row_start, block_rows, 0)
    key_segments = lax.dynamic_slice_in_dim(segments_padded, row_start, window_rows, 0)
    query_places = row_start + jnp.arange(block_rows, dtype=jnp.int32)
    key_places = row_start - SPAN * block_rows + jnp.arange(window_rows, dtype=jnp.int32)
    allowed = (query_segments[:, None] == key_segments[None, :]) & (
        key_places[None, :] <= query_places[:, None]
    )
    first_segment = query_segments[0]
    doc_start = jnp.sum((segment_ids < first_segment).astype(jnp.int32))
    reach_back = jnp.clip(owner - doc_start // block_rows, 0, SPAN)
    return (allowed, reach_back)


def attend_rows(query_rows, grad_rows, key_window, value_window, allowed):
    row_count = query_rows.shape[0]
    head_dim = query_rows.shape[2]
    kv_groups = key_window.shape[1]
    group_size = query_rows.shape[1] // kv_groups
    pair_count = group_size // 2
    window_rows = key_window.shape[0]
    score_scale = 1.0 / math.sqrt(head_dim)
    query_pairs = query_rows.reshape(row_count, kv_groups * pair_count, 2, head_dim).transpose(
        1, 0, 2, 3
    )
    grad_pairs = grad_rows.reshape(row_count, kv_groups * pair_count, 2, head_dim).transpose(
        1, 0, 2, 3
    )

    def head_step(running, inputs):
        key_sums, value_sums = running
        pair_index, query_pair, grad_pair = inputs
        kv_group = pair_index // pair_count
        key_rows = lax.dynamic_index_in_dim(key_window, kv_group, 1, keepdims=False)
        value_rows = lax.dynamic_index_in_dim(value_window, kv_group, 1, keepdims=False)
        results = tile_math(query_pair, grad_pair, key_rows, value_rows, allowed, score_scale)
        attended, grad_query, grad_key, grad_value = results
        key_sums = key_sums.at[:, kv_group].add(grad_key)
        value_sums = value_sums.at[:, kv_group].add(grad_value)
        return ((key_sums, value_sums), (attended, grad_query))

    zero_sums = jnp.zeros((window_rows, kv_groups, head_dim), jnp.float32)
    (key_sums, value_sums), (attended_all, grad_all) = lax.scan(
        head_step,
        (zero_sums, zero_sums),
        (jnp.arange(kv_groups * pair_count, dtype=jnp.int32), query_pairs, grad_pairs),
    )
    attention = attended_all.transpose(1, 0, 2, 3).reshape(
        row_count, kv_groups * group_size, head_dim
    )
    grad_queries = grad_all.transpose(1, 0, 2, 3).reshape(
        row_count, kv_groups * group_size, head_dim
    )
    return (attention, grad_queries, key_sums, value_sums)


def local(queries, keys, values, grad_out, segment_ids):
    query_local, grad_local, key_local, value_local = (
        lax.all_to_all(queries, "kvh", split_axis=1, concat_axis=0, tiled=True),
        lax.all_to_all(grad_out, "kvh", split_axis=1, concat_axis=0, tiled=True),
        lax.all_to_all(keys, "kvh", split_axis=1, concat_axis=0, tiled=True),
        lax.all_to_all(values, "kvh", split_axis=1, concat_axis=0, tiled=True),
    )
    block_rows = query_local.shape[0]
    position = lax.axis_index("ctx")
    earlier = []
    for distance in range(SPAN, 0, -1):
        earlier.append(passed_along((key_local, value_local), "ctx", distance))
    key_window = jnp.concatenate([piece[0] for piece in earlier] + [key_local], axis=0)
    value_window = jnp.concatenate([piece[1] for piece in earlier] + [value_local], axis=0)
    window_rows = key_window.shape[0]
    allowed, reach_back = window_mask(segment_ids, position, block_rows, window_rows)
    attention, grad_queries, key_sums, value_sums = attend_rows(
        query_local, grad_local, key_window, value_window, allowed
    )

    def key_piece(distance):
        return key_sums[(SPAN - distance) * block_rows : (SPAN - distance + 1) * block_rows]

    def value_piece(distance):
        return value_sums[(SPAN - distance) * block_rows : (SPAN - distance + 1) * block_rows]

    summed_keys = key_piece(0)
    summed_values = value_piece(0)
    for distance in range(1, SPAN + 1):
        arrived = passed_along((key_piece(distance), value_piece(distance)), "ctx", -distance)
        summed_keys = summed_keys + arrived[0]
        summed_values = summed_values + arrived[1]
    return (
        attention,
        grad_queries,
        summed_keys.astype(jnp.bfloat16),
        summed_values.astype(jnp.bfloat16),
    )


def solution(mesh):
    return jax.shard_map(
        local,
        mesh=mesh,
        in_specs=(
            P(("ctx", "kvh"), None, None),
            P(("ctx", "kvh"), None, None),
            P(("ctx", "kvh"), None, None),
            P(("ctx", "kvh"), None, None),
            P(),
        ),
        out_specs=(
            P("ctx", "kvh", None),
            P("ctx", "kvh", None),
            P("ctx", "kvh", None),
            P("ctx", "kvh", None),
        ),
        check_vma=False,
    )
```

profile of v0, /device:TPU:250, one launch (start us, length us, event | category | flops | bytes accessed | tf_op | source)
XLA Modules:
  0.0 199.3 jit_solution(17445718715498427000)
XLA Ops:
  2.2 5.7 %all-to-all-start.1 = ((bf16[48,8,128]{2,0,1:T(8,128)(2,1)}), bf16[48,8,128]{2,0,1:T(8,128)(2,1)S(1)}, u32[]{:S(2)}, u32[]{:S(2)}) async-start(bf16[48,8,128]{2,0,1:T(8,128)(2,1)} %copy.21), calls=%async_computation.1 | async-start | bytes 196608 | tf_op jit(solution)/shard_map/all_to_all | solution.py:110
  9.5 2.8 %all-to-all-done.1 = bf16[48,8,128]{2,0,1:T(8,128)(2,1)S(1)} async-done(((bf16[48,8,128]{2,0,1:T(8,128)(2,1)}), bf16[48,8,128]{2,0,1:T(8,128)(2,1)S(1)}, u32[]{:S(2)}, u32[]{:S(2)}) %all-to-all-start.1) | async-done | bytes 98336 | tf_op jit(solution)/shard_map/all_to_all | solution.py:110
  12.3 5.5 %all-to-all-start.3 = ((bf16[48,8,128]{2,0,1:T(8,128)(2,1)}), bf16[48,8,128]{2,0,1:T(8,128)(2,1)S(1)}, u32[]{:S(2)}, u32[]{:S(2)}) async-start(bf16[48,8,128]{2,0,1:T(8,128)(2,1)} %copy.24), calls=%async_computation.3 | async-start | bytes 196608 | tf_op jit(solution)/shard_map/all_to_all | solution.py:111
  17.8 2.5 %copy.19 = bf16[48,64,128]{2,0,1:T(8,128)(2,1)} copy(bf16[48,64,128]{2,1,0:T(8,128)(2,1)} %param.11) | data formatting | bytes 1572864 | tf_op args[0]
  22.1 5.7 %all-to-all-start = ((bf16[48,64,128]{2,0,1:T(8,128)(2,1)}), bf16[48,64,128]{2,0,1:T(8,128)(2,1)S(1)}, u32[]{:S(2)}, u32[]{:S(2)}) async-start(bf16[48,64,128]{2,0,1:T(8,128)(2,1)} %copy.19), calls=%async_computation | async-start | bytes 1572864 | tf_op jit(solution)/shard_map/all_to_all | solution.py:108
  27.8 2.5 %copy.22 = bf16[48,64,128]{2,0,1:T(8,128)(2,1)} copy(bf16[48,64,128]{2,1,0:T(8,128)(2,1)} %param.14) | data formatting | bytes 1572864 | tf_op args[3]
  30.3 6.0 %all-to-all-done = bf16[48,64,128]{2,0,1:T(8,128)(2,1)S(1)} async-done(((bf16[48,64,128]{2,0,1:T(8,128)(2,1)}), bf16[48,64,128]{2,0,1:T(8,128)(2,1)S(1)}, u32[]{:S(2)}, u32[]{:S(2)}) %all-to-all-start) | async-done | bytes 786464 | tf_op jit(solution)/shard_map/all_to_all | solution.py:108
  36.4 6.3 %all-to-all-start.2 = ((bf16[48,64,128]{2,0,1:T(8,128)(2,1)}), bf16[48,64,128]{2,0,1:T(8,128)(2,1)}, u32[]{:S(2)}, u32[]{:S(2)}) async-start(bf16[48,64,128]{2,0,1:T(8,128)(2,1)} %copy.22), calls=%async_computation.2 | async-start | bytes 1572864 | tf_op jit(solution)/shard_map/all_to_all | solution.py:109
  45.3 5.6 %collective-permute-start.4 = (bf16[384,1,128]{2,0,1:T(8,128)(2,1)S(1)}, bf16[384,1,128]{2,0,1:T(8,128)(2,1)S(1)}, u32[]{:S(2)}, u32[]{:S(2)}) collective-permute-start(bf16[384,1,128]{2,0,1:T(8,128)(2,1)S(1)} %bitcast.168), channel_id=1, source_target_pairs={{0,16},{8,24},{16,32},{24,40},{32,48},{40,56},{48,64},{56,72},{64,... | collective-permute-start | bytes 294920 | tf_op jit(solution)/shard_map/ppermute | solution.py:14
  50.9 4.5 %collective-permute-start.3 = (bf16[384,1,128]{2,0,1:T(8,128)(2,1)S(1)}, bf16[384,1,128]{2,0,1:T(8,128)(2,1)S(1)}, u32[]{:S(2)}, u32[]{:S(2)}) collective-permute-start(bf16[384,1,128]{2,0,1:T(8,128)(2,1)S(1)} %bitcast.169), channel_id=1, source_target_pairs={{0,24},{8,32},{16,40},{24,48},{32,56},{40,64},{48,72},{56,80},{64,... | collective-permute-start | bytes 294920 | tf_op jit(solution)/shard_map/ppermute | solution.py:14
  58.0 3.5 %collective-permute-start.1 = (bf16[384,1,128]{2,0,1:T(8,128)(2,1)S(1)}, bf16[384,1,128]{2,0,1:T(8,128)(2,1)S(1)}, u32[]{:S(2)}, u32[]{:S(2)}) collective-permute-start(bf16[384,1,128]{2,0,1:T(8,128)(2,1)S(1)} %bitcast.164), channel_id=1, source_target_pairs={{0,16},{8,24},{16,32},{24,40},{32,48},{40,56},{48,64},{56,72},{64,... | collective-permute-start | bytes 294920 | tf_op jit(solution)/shard_map/ppermute | solution.py:14
  61.5 4.7 %collective-permute-start = (bf16[384,1,128]{2,0,1:T(8,128)(2,1)S(1)}, bf16[384,1,128]{2,0,1:T(8,128)(2,1)S(1)}, u32[]{:S(2)}, u32[]{:S(2)}) collective-permute-start(bf16[384,1,128]{2,0,1:T(8,128)(2,1)S(1)} %bitcast.165), channel_id=1, source_target_pairs={{0,24},{8,32},{16,40},{24,48},{32,56},{40,64},{48,72},{56,80},{64,... | collective-permute-start | bytes 294920 | tf_op jit(solution)/shard_map/ppermute | solution.py:14
  66.3 4.0 %collective-permute-done = bf16[384,1,128]{2,0,1:T(8,128)(2,1)S(1)} collective-permute-done((bf16[384,1,128]{2,0,1:T(8,128)(2,1)S(1)}, bf16[384,1,128]{2,0,1:T(8,128)(2,1)S(1)}, u32[]{:S(2)}, u32[]{:S(2)}) %collective-permute-start) | collective-permute-done | bytes 98336 | tf_op jit(solution)/shard_map/ppermute | solution.py:14
  72.9 66.9 %while.21 = (s32[]{:T(128)}, f32[1536,1,128]{2,0,1:T(8,128)S(1)}, f32[1536,1,128]{2,0,1:T(8,128)S(1)}, bf16[4,384,2,128]{3,1,2,0:T(8,128)(2,1)}, bf16[4,384,2,12...) while((s32[]{:T(128)}, f32[1536,1,128]{2,0,1:T(8,128)S(1)}, ...), condition=%wide.region_5.6_spmd.clone, body=%wide.region_0.5_spmd.clone.sunk | while | flops 1831991808 | bytes 40157636 | solution.py:92
  111.8 2.2 %bitcast_reduce_fusion.2 = (f32[2,384]{1,0:T(2,128)S(1)}, f32[384,2,1536]{2,0,1:T(8,128)S(1)}) fusion(bf16[1536,1,128]{2,0,1:T(8,128)(2,1)} %get-tuple-element.398, bf16[4,384,2,128]{3,1,2,0:T(8,128)(2,1)S(1)} %get-tuple-element.397, s32[]{:T(128)S(6)} %copy.36, pred[384,1536]{1,0:T(8,128)(4,1)S(1)} %compare_and_fusion.2), kind=kOutput, calls=%fused_computation.7.clone.1 | convolution fusion | flops 305528064 | bytes 5901316 | tf_op jit(solution)/shard_map/while/body/eval_jaxpr/bhd,wd->hbw/dot_general | solution.py:19
  128.5 2.2 %bitcast_reduce_fusion.2 = (f32[2,384]{1,0:T(2,128)S(1)}, f32[384,2,1536]{2,0,1:T(8,128)S(1)}) fusion(bf16[1536,1,128]{2,0,1:T(8,128)(2,1)} %get-tuple-element.398, bf16[4,384,2,128]{3,1,2,0:T(8,128)(2,1)S(1)} %get-tuple-element.397, s32[]{:T(128)S(6)} %copy.36, pred[384,1536]{1,0:T(8,128)(4,1)S(1)} %compare_and_fusion.2), kind=kOutput, calls=%fused_computation.7.clone.1 | convolution fusion | flops 305528064 | bytes 5901316 | tf_op jit(solution)/shard_map/while/body/eval_jaxpr/bhd,wd->hbw/dot_general | solution.py:19
  139.8 2.8 %copy.26 = bf16[384,4,2,128]{3,2,1,0:T(2,128)(2,1)} copy(bf16[384,4,2,128]{3,0,2,1:T(8,128)(2,1)} %bitcast.159) | data formatting | bytes 1572864 | tf_op jit(solution)/shard_map/transpose | solution.py:100
  142.6 2.8 %copy.25 = bf16[384,4,2,128]{3,2,1,0:T(2,128)(2,1)} copy(bf16[384,4,2,128]{3,0,2,1:T(8,128)(2,1)} %bitcast.160) | data formatting | bytes 1572864 | tf_op jit(solution)/shard_map/transpose | solution.py:97
  147.5 3.3 %collective-permute-start.8 = (f32[384,1,128]{2,0,1:T(8,128)S(1)}, f32[384,1,128]{2,0,1:T(8,128)S(1)}, u32[]{:S(2)}, u32[]{:S(2)}) collective-permute-start(f32[384,1,128]{2,0,1:T(8,128)S(1)} %get-tuple-element.258), channel_id=1, source_target_pairs={{24,0},{32,8},{40,16},{48,24},{56,32},{64,40},{72,48},{80,56},{88,... | collective-permute-start | bytes 589832 | tf_op jit(solution)/shard_map/ppermute | solution.py:14
  157.1 5.0 %collective-permute-start.10 = (f32[384,1,128]{2,0,1:T(8,128)S(1)}, f32[384,1,128]{2,0,1:T(8,128)S(1)}, u32[]{:S(2)}, u32[]{:S(2)}) collective-permute-start(f32[384,1,128]{2,0,1:T(8,128)S(1)} %get-tuple-element.256), channel_id=1, source_target_pairs={{16,0},{24,8},{32,16},{40,24},{48,32},{56,40},{64,48},{72,56},{80,... | collective-permute-start | bytes 589832 | tf_op jit(solution)/shard_map/ppermute | solution.py:14
  162.1 7.8 %collective-permute-done.8 = f32[384,1,128]{2,0,1:T(8,128)S(1)} collective-permute-done((f32[384,1,128]{2,0,1:T(8,128)S(1)}, f32[384,1,128]{2,0,1:T(8,128)S(1)}, u32[]{:S(2)}, u32[]{:S(2)}) %collective-permute-start.8) | collective-permute-done | bytes 196640 | tf_op jit(solution)/shard_map/ppermute | solution.py:14
  169.9 13.4 %collective-permute-done.7 = f32[384,1,128]{2,0,1:T(8,128)S(1)} collective-permute-done((f32[384,1,128]{2,0,1:T(8,128)S(1)}, f32[384,1,128]{2,0,1:T(8,128)S(1)}, u32[]{:S(2)}, u32[]{:S(2)}) %collective-permute-start.7) | collective-permute-done | bytes 196640 | tf_op jit(solution)/shard_map/ppermute | solution.py:14
  184.1 6.5 %collective-permute-done.11 = f32[384,1,128]{2,0,1:T(8,128)S(1)} collective-permute-done((f32[384,1,128]{2,0,1:T(8,128)S(1)}, f32[384,1,128]{2,0,1:T(8,128)S(1)}, u32[]{:S(2)}, u32[]{:S(2)}) %collective-permute-start.11) | collective-permute-done | bytes 196640 | tf_op jit(solution)/shard_map/ppermute | solution.py:14
  190.6 8.0 %collective-permute-done.10 = f32[384,1,128]{2,0,1:T(8,128)S(1)} collective-permute-done((f32[384,1,128]{2,0,1:T(8,128)S(1)}, f32[384,1,128]{2,0,1:T(8,128)S(1)}, u32[]{:S(2)}, u32[]{:S(2)}) %collective-permute-start.10) | collective-permute-done | bytes 196640 | tf_op jit(solution)/shard_map/ppermute | solution.py:14
  (93 shorter events, 75.8 us)
Async XLA Ops:
  0.6 42.0 %copy-start.1 = (s32[24576]{0:T(1024)S(1)}, s32[24576]{0:T(1024)}, u32[]{:S(2)}) copy-start(s32[24576]{0:T(1024)} %param.15) | copy-start | bytes 294916
  2.2 10.1 %all-to-all-start.1 = ((bf16[48,8,128]{2,0,1:T(8,128)(2,1)}), bf16[48,8,128]{2,0,1:T(8,128)(2,1)S(1)}, u32[]{:S(2)}, u32[]{:S(2)}) async-start(bf16[48,8,128]{2,0,1:T(8,128)(2,1)} %copy.21), calls=%async_computation.1 | async-start | bytes 196608 | tf_op jit(solution)/shard_map/all_to_all | solution.py:110
  12.3 9.8 %all-to-all-start.3 = ((bf16[48,8,128]{2,0,1:T(8,128)(2,1)}), bf16[48,8,128]{2,0,1:T(8,128)(2,1)S(1)}, u32[]{:S(2)}, u32[]{:S(2)}) async-start(bf16[48,8,128]{2,0,1:T(8,128)(2,1)} %copy.24), calls=%async_computation.3 | async-start | bytes 196608 | tf_op jit(solution)/shard_map/all_to_all | solution.py:111
  22.1 14.2 %all-to-all-start = ((bf16[48,64,128]{2,0,1:T(8,128)(2,1)}), bf16[48,64,128]{2,0,1:T(8,128)(2,1)S(1)}, u32[]{:S(2)}, u32[]{:S(2)}) async-start(bf16[48,64,128]{2,0,1:T(8,128)(2,1)} %copy.19), calls=%async_computation | async-start | bytes 1572864 | tf_op jit(solution)/shard_map/all_to_all | solution.py:108
  36.4 34.7 %all-to-all-start.2 = ((bf16[48,64,128]{2,0,1:T(8,128)(2,1)}), bf16[48,64,128]{2,0,1:T(8,128)(2,1)}, u32[]{:S(2)}, u32[]{:S(2)}) async-start(bf16[48,64,128]{2,0,1:T(8,128)(2,1)} %copy.22), calls=%async_computation.2 | async-start | bytes 1572864 | tf_op jit(solution)/shard_map/all_to_all | solution.py:109
  43.4 18.1 %collective-permute-start.5 = (bf16[384,1,128]{2,0,1:T(8,128)(2,1)S(1)}, bf16[384,1,128]{2,0,1:T(8,128)(2,1)S(1)}, u32[]{:S(2)}, u32[]{:S(2)}) collective-permute-start(bf16[384,1,128]{2,0,1:T(8,128)(2,1)S(1)} %bitcast.167), channel_id=1, source_target_pairs={{0,8},{8,16},{16,24},{24,32},{32,40},{40,48},{48,56},{56,64},{64,7... | collective-permute-start | bytes 294920 | tf_op jit(solution)/shard_map/ppermute | solution.py:14
  45.3 20.9 %collective-permute-start.4 = (bf16[384,1,128]{2,0,1:T(8,128)(2,1)S(1)}, bf16[384,1,128]{2,0,1:T(8,128)(2,1)S(1)}, u32[]{:S(2)}, u32[]{:S(2)}) collective-permute-start(bf16[384,1,128]{2,0,1:T(8,128)(2,1)S(1)} %bitcast.168), channel_id=1, source_target_pairs={{0,16},{8,24},{16,32},{24,40},{32,48},{40,56},{48,64},{56,72},{64,... | collective-permute-start | bytes 294920 | tf_op jit(solution)/shard_map/ppermute | solution.py:14
  50.9 15.3 %collective-permute-start.3 = (bf16[384,1,128]{2,0,1:T(8,128)(2,1)S(1)}, bf16[384,1,128]{2,0,1:T(8,128)(2,1)S(1)}, u32[]{:S(2)}, u32[]{:S(2)}) collective-permute-start(bf16[384,1,128]{2,0,1:T(8,128)(2,1)S(1)} %bitcast.169), channel_id=1, source_target_pairs={{0,24},{8,32},{16,40},{24,48},{32,56},{40,64},{48,72},{56,80},{64,... | collective-permute-start | bytes 294920 | tf_op jit(solution)/shard_map/ppermute | solution.py:14
  56.0 10.3 %collective-permute-start.2 = (bf16[384,1,128]{2,0,1:T(8,128)(2,1)S(1)}, bf16[384,1,128]{2,0,1:T(8,128)(2,1)S(1)}, u32[]{:S(2)}, u32[]{:S(2)}) collective-permute-start(bf16[384,1,128]{2,0,1:T(8,128)(2,1)S(1)} %bitcast.163), channel_id=1, source_target_pairs={{0,8},{8,16},{16,24},{24,32},{32,40},{40,48},{48,56},{56,64},{64,7... | collective-permute-start | bytes 294920 | tf_op jit(solution)/shard_map/ppermute | solution.py:14
  58.0 8.3 %collective-permute-start.1 = (bf16[384,1,128]{2,0,1:T(8,128)(2,1)S(1)}, bf16[384,1,128]{2,0,1:T(8,128)(2,1)S(1)}, u32[]{:S(2)}, u32[]{:S(2)}) collective-permute-start(bf16[384,1,128]{2,0,1:T(8,128)(2,1)S(1)} %bitcast.164), channel_id=1, source_target_pairs={{0,16},{8,24},{16,32},{24,40},{32,48},{40,56},{48,64},{56,72},{64,... | collective-permute-start | bytes 294920 | tf_op jit(solution)/shard_map/ppermute | solution.py:14
  61.5 8.7 %collective-permute-start = (bf16[384,1,128]{2,0,1:T(8,128)(2,1)S(1)}, bf16[384,1,128]{2,0,1:T(8,128)(2,1)S(1)}, u32[]{:S(2)}, u32[]{:S(2)}) collective-permute-start(bf16[384,1,128]{2,0,1:T(8,128)(2,1)S(1)} %bitcast.165), channel_id=1, source_target_pairs={{0,24},{8,32},{16,40},{24,48},{32,56},{40,64},{48,72},{56,80},{64,... | collective-permute-start | bytes 294920 | tf_op jit(solution)/shard_map/ppermute | solution.py:14
  86.4 1.8 copy-start
  103.1 1.8 copy-start
  119.8 1.8 copy-start
  136.5 1.8 copy-start
  145.5 11.6 %collective-permute-start.6 = (f32[384,1,128]{2,0,1:T(8,128)S(1)}, f32[384,1,128]{2,0,1:T(8,128)S(1)}, u32[]{:S(2)}, u32[]{:S(2)}) collective-permute-start(f32[384,1,128]{2,0,1:T(8,128)S(1)} %get-tuple-element.257), channel_id=1, source_target_pairs={{8,0},{16,8},{24,16},{32,24},{40,32},{48,40},{56,48},{64,56},{72,6... | collective-permute-start | bytes 589832 | tf_op jit(solution)/shard_map/ppermute | solution.py:14
  147.5 22.4 %collective-permute-start.8 = (f32[384,1,128]{2,0,1:T(8,128)S(1)}, f32[384,1,128]{2,0,1:T(8,128)S(1)}, u32[]{:S(2)}, u32[]{:S(2)}) collective-permute-start(f32[384,1,128]{2,0,1:T(8,128)S(1)} %get-tuple-element.258), channel_id=1, source_target_pairs={{24,0},{32,8},{40,16},{48,24},{56,32},{64,40},{72,48},{80,56},{88,... | collective-permute-start | bytes 589832 | tf_op jit(solution)/shard_map/ppermute | solution.py:14
  150.9 32.5 %collective-permute-start.7 = (f32[384,1,128]{2,0,1:T(8,128)S(1)}, f32[384,1,128]{2,0,1:T(8,128)S(1)}, u32[]{:S(2)}, u32[]{:S(2)}) collective-permute-start(f32[384,1,128]{2,0,1:T(8,128)S(1)} %get-tuple-element.259), channel_id=1, source_target_pairs={{16,0},{24,8},{32,16},{40,24},{48,32},{56,40},{64,48},{72,56},{80,... | collective-permute-start | bytes 589832 | tf_op jit(solution)/shard_map/ppermute | solution.py:14
  152.9 31.1 %collective-permute-start.9 = (f32[384,1,128]{2,0,1:T(8,128)S(1)}, f32[384,1,128]{2,0,1:T(8,128)S(1)}, u32[]{:S(2)}, u32[]{:S(2)}) collective-permute-start(f32[384,1,128]{2,0,1:T(8,128)S(1)} %get-tuple-element.254), channel_id=1, source_target_pairs={{8,0},{16,8},{24,16},{32,24},{40,32},{48,40},{56,48},{64,56},{72,6... | collective-permute-start | bytes 589832 | tf_op jit(solution)/shard_map/ppermute | solution.py:14
  155.1 35.5 %collective-permute-start.11 = (f32[384,1,128]{2,0,1:T(8,128)S(1)}, f32[384,1,128]{2,0,1:T(8,128)S(1)}, u32[]{:S(2)}, u32[]{:S(2)}) collective-permute-start(f32[384,1,128]{2,0,1:T(8,128)S(1)} %get-tuple-element.255), channel_id=1, source_target_pairs={{24,0},{32,8},{40,16},{48,24},{56,32},{64,40},{72,48},{80,56},{88,... | collective-permute-start | bytes 589832 | tf_op jit(solution)/shard_map/ppermute | solution.py:14
  157.1 41.6 %collective-permute-start.10 = (f32[384,1,128]{2,0,1:T(8,128)S(1)}, f32[384,1,128]{2,0,1:T(8,128)S(1)}, u32[]{:S(2)}, u32[]{:S(2)}) collective-permute-start(f32[384,1,128]{2,0,1:T(8,128)S(1)} %get-tuple-element.256), channel_id=1, source_target_pairs={{16,0},{24,8},{32,16},{40,24},{48,32},{56,40},{64,48},{72,56},{80,... | collective-permute-start | bytes 589832 | tf_op jit(solution)/shard_map/ppermute | solution.py:14
where the time goes:
time: 201 us; the launch traced here: 199 us
  starting transfers between devices  61.9 us (31%)
  waiting for transfers between devices  50.4 us (25%)
  matrix products  37.9 us (19%)
  local copies, waits for them, and re-layouts  24.2 us (12%)
  other arithmetic  14.8 us (7%)
  loops' own time  9.28 us (5%)
    ppermute x12, waiting for transfers between devices, passed_along(): lax.ppermute(value, axis, [(source, source + steps) for source in range(l...  39.8 us
    ppermute x12, starting transfers between devices, passed_along(): lax.ppermute(value, axis, [(source, source + steps) for source in range(l...  38.8 us
    another operation x1, loops' own time, attend_rows(): lax.scan(head_step, (zero_sums, zero_sums), (jnp.arange(kv_groups * pair_...  9.28 us
    dot_general x4, matrix products, tile_math(): jnp.einsum('bhd,wd->hbw', query_pair, key_rows, preferred_element_type=jn...  8.78 us
    unnamed x6, local copies, waits for them, and re-layouts  8.18 us
    dot_general x4, matrix products, tile_math(): jnp.einsum('hbw,bhd->wd', probs_low, grad_pair, preferred_element_type=jn...  7.83 us
    dot_general x4, matrix products, tile_math(): jnp.einsum('hbw,bhd->wd', grad_scores, query_pair, preferred_element_type...  7.02 us
    all_to_all x1, starting transfers between devices, local(): lax.all_to_all(grad_out, 'kvh', split_axis=1, concat_axis=0, tiled=True)  6.27 us
  transfers between devices with their start and end apart: 16, of which 8 were waited for; matrix products, arithmetic and copies ran while one was open for 5% of the time, Pallas kernels for 0%

commit v1 on v0

v1 whole, which is shorter than its diff:
```python
import functools
import math

import jax
import jax.numpy as jnp
from jax import lax
from jax.experimental import pallas as pl
from jax.experimental.pallas import tpu as pltpu
from jax.sharding import PartitionSpec as P

MESH = pl.DeviceIdType.MESH
SPAN = 3
BIG = 1e30
F32 = jnp.float32
BF16 = jnp.bfloat16

ROWS = 384
PIECE = 48
GROUPS = 8
QPK = 8
DIM = 128
PAIR = 2 * PIECE
PAIRS = ROWS // PAIR
COLS = PAIR * QPK
WINDOW = (SPAN + 1) * ROWS
BAND = SPAN * ROWS + PAIR
SCALE = 1.0 / math.sqrt(DIM)
LOG2E = math.log2(math.e)

NT = (((1,), (1,)), ((), ()))
TN = (((0,), (0,)), ((), ()))
NN = (((1,), (0,)), ((), ()))


def dot(a, b, dims):
    return lax.dot_general(a, b, dims, preferred_element_type=F32)


def kernel(
    n_ctx,
    q_ref, do_ref, k_ref, v_ref, seg_ref,
    att_ref, dq_ref, dk_ref, dv_ref,
    stage, kvsend, kvwin, ohk, ohq, qbuf, dobuf, qm, dom, doms, s_ref, p_all, delta, rls,
    dqt, dk_acc, dv_acc, gsend, grecv,
    a2a_send, a2a_recv, fwd_send, fwd_recv, g_send, g_recv,
):
    c = lax.axis_index("ctx")
    g = lax.axis_index("kvh")
    x = g // 2
    odd = lax.rem(c, 2)
    sibling = c + 1 - 2 * odd

    def along(steps):
        return lax.rem(c + (steps + n_ctx), n_ctx)

    barrier = pltpu.get_barrier_semaphore()
    for s in range(1, GROUPS):
        pl.semaphore_signal(
            barrier, inc=1, device_id=(c, lax.rem(g + s, GROUPS)), device_id_type=MESH
        )
    for steps in (1, -1, 2, -2):
        pl.semaphore_signal(barrier, inc=1, device_id=(along(steps), g), device_id_type=MESH)

    for i, ref in enumerate((k_ref, v_ref)):
        stage[...] = ref[...].astype(F32).reshape(PIECE * GROUPS, DIM)
        for h in range(GROUPS):
            kvsend[h, i] = stage[pl.ds(h, PIECE, stride=GROUPS), :].astype(BF16)

    pl.semaphore_wait(barrier, GROUPS - 1 + 4)

    own = SPAN * ROWS
    my_rows = pl.ds(pl.multiple_of(g * PIECE, PIECE), PIECE)

    def kv_slot(i):
        return kvwin.at[i, pl.ds(pl.multiple_of(own + g * PIECE, PIECE), PIECE)]

    def kv_copy(i, peer, slot):
        return pltpu.make_async_remote_copy(
            src_ref=kvsend.at[peer, i], dst_ref=kv_slot(i),
            send_sem=a2a_send.at[i, slot], recv_sem=a2a_recv.at[i, g],
            device_id=(c, peer), device_id_type=MESH,
        )

    def wide_copy(i, src, dst, peer, slot):
        return pltpu.make_async_remote_copy(
            src_ref=src.at[:, peer], dst_ref=dst.at[my_rows],
            send_sem=a2a_send.at[i, slot], recv_sem=a2a_recv.at[i, g],
            device_id=(c, peer), device_id_type=MESH,
        )

    peers = []
    z = lax.rem(g, 2)
    for step in (0, 1, 3, 2):
        px = lax.rem(x + step, PAIRS)
        for other in (0, 1):
            if step == 0 and other == 0:
                continue
            peers.append(2 * px + lax.rem(z + other, 2))

    for i in range(2):
        for slot, peer in enumerate(peers):
            kv_copy(i, peer, slot).start()
        pltpu.make_async_copy(kvsend.at[g, i], kv_slot(i), a2a_recv.at[i, g]).start()
    pltpu.make_async_copy(q_ref.at[:, g], qbuf.at[my_rows], a2a_recv.at[2, g]).start()
    pltpu.make_async_copy(do_ref.at[:, g], dobuf.at[my_rows], a2a_recv.at[3, g]).start()
    for slot, peer in enumerate(peers):
        wide_copy(2, q_ref, qbuf, peer, slot).start()
        wide_copy(3, do_ref, dobuf, peer, slot).start()

    def arrived(ref, sem):
        pltpu.make_async_copy(ref, ref, sem).wait()

    tiles = WINDOW // DIM
    seg_rows = n_ctx * ROWS // DIM
    first = c * (ROWS // DIM) + seg_rows - SPAN * (ROWS // DIM)
    number = lax.broadcasted_iota(jnp.int32, (DIM, DIM), 0)
    for i in range(tiles):
        row = seg_ref[pl.ds(lax.rem(first + i, seg_rows), 1), :]
        hot = jnp.where(number == row, 1.0, 0.0).T
        ohk[i * DIM : (i + 1) * DIM, :] = hot.astype(BF16)
        if i >= tiles - ROWS // DIM:
            at = (i - (tiles - ROWS // DIM)) * DIM
            ohq[at : at + DIM, :] = (hot - 1.0) * BIG
    dk_acc[...] = jnp.zeros_like(dk_acc)
    dv_acc[...] = jnp.zeros_like(dv_acc)
    dqt[...] = jnp.zeros_like(dqt)

    def block(i, d):
        return kvwin.at[i, pl.ds(own - d * ROWS, ROWS)]

    def fwd_copy(i, n, src, d, there):
        return pltpu.make_async_remote_copy(
            src_ref=src, dst_ref=block(i, d),
            send_sem=fwd_send.at[i, n], recv_sem=fwd_recv.at[i, d - 1],
            device_id=(there, g), device_id_type=MESH,
        )

    def to_two(i):
        return fwd_copy(i, 0, block(i, 0), 2, along(2))

    def to_sibling(i, d):
        return fwd_copy(i, 1, block(i, d), 1, sibling)

    def to_three(i):
        return fwd_copy(i, 2, block(i, 2), 3, along(1))

    for i in range(2):
        for j in range(GROUPS):
            arrived(kvwin.at[i, pl.ds(own + j * PIECE, PIECE)], a2a_recv.at[i, j])
        to_two(i).start()

        @pl.when(odd == 0)
        def _():
            to_sibling(i, 0).start()

    for i in range(2):
        arrived(block(i, 2), fwd_recv.at[i, 1])
        to_three(i).start()

        @pl.when(odd == 1)
        def _():
            to_sibling(i, 2).start()

    for d in (1, 3):
        arrived(block(0, d), fwd_recv.at[0, d - 1])

    def forward(t, carry):
        step = jnp.where(t == 0, 0, jnp.where(t == 1, 3, jnp.where(t == 2, 1, 2)))
        jj = lax.rem(x + step, PAIRS)
        base = pl.multiple_of(jj * PAIR, PAIR)
        rows = pl.ds(base, PAIR)
        for half in range(2):
            piece = pl.ds(pl.multiple_of(base + half * PIECE, PIECE), PIECE)
            arrived(qbuf.at[piece], a2a_recv.at[2, 2 * jj + half])
            arrived(dobuf.at[piece], a2a_recv.at[3, 2 * jj + half])
        qf = qbuf[rows].astype(F32).reshape(COLS, DIM)
        qb = qf.astype(BF16)
        penalty = jnp.broadcast_to(ohq[rows, :][:, None, :], (PAIR, QPK, DIM))
        qa = jnp.concatenate([qb, penalty.reshape(COLS, DIM).astype(BF16)], axis=1)
        part = BAND // 3
        m8 = None
        for ch in range(3):
            keys = pl.ds(pl.multiple_of(base + ch * part, 32), part)
            ka = jnp.concatenate([kvwin[0, keys, :], ohk[keys, :]], axis=1)
            s = dot(ka, qa, NT)
            if ch == 2:
                tail = s[part - PAIR :]
                key_at = lax.broadcasted_iota(jnp.int32, (PAIR, COLS), 0) * QPK
                col_at = lax.broadcasted_iota(jnp.int32, (PAIR, COLS), 1)
                tail = jnp.where(key_at <= col_at, tail, -BIG)
                s = jnp.concatenate([s[: part - PAIR], tail], axis=0)
            s_ref[ch * part : (ch + 1) * part, :] = s
            top = jnp.max(s.reshape(part // 8, 8, COLS), axis=0)
            m8 = top if m8 is None else jnp.maximum(m8, top)
        m = jnp.max(m8, axis=0, keepdims=True)
        l8 = jnp.zeros((8, COLS), F32)
        for ch in range(BAND // PAIR):
            at = slice(ch * PAIR, (ch + 1) * PAIR)
            e = jnp.exp2((s_ref[at, :] - m) * (SCALE * LOG2E))
            l8 = l8 + jnp.sum(e.reshape(PAIR // 8, 8, COLS), axis=0)
            p_all[jj, at, :] = e.astype(BF16)
        rl = 1.0 / jnp.sum(l8, axis=0, keepdims=True)
        rls[jj] = rl
        by_row = jnp.broadcast_to(rl, (DIM, COLS)).T
        qm[jj] = (qf * by_row).astype(BF16)
        dof = dobuf[rows].astype(F32).reshape(COLS, DIM)
        dom[jj] = dof.astype(BF16)
        doms[jj] = (dof * by_row).astype(BF16)

        @pl.when(t == 0)
        def _():
            for d in (1, 3):
                arrived(block(1, d), fwd_recv.at[1, d - 1])

        band = pl.ds(base, BAND)
        ot = dot(kvwin[1, band, :], p_all[jj], TN) * rl
        ot = ot.astype(BF16).astype(F32)
        att_ref[rows] = ot.T.reshape(PAIR, QPK, DIM).astype(BF16)
        delta[jj] = jnp.sum(dof.T * ot, axis=0, keepdims=True)
        return carry

    lax.fori_loop(0, PAIRS, forward, 0)

    def unit(jj, key_lo, size, off):
        keys = slice(key_lo, key_lo + size)
        ks = kvwin[0, keys, :]
        p = p_all[jj, pl.ds(off, size), :]
        dpt = dot(kvwin[1, keys, :], dom[jj], NT)
        ds = p * (dpt - delta[jj]).astype(BF16)
        dv_acc[keys, :] += dot(p, doms[jj], NN)
        dk_acc[keys, :] += dot(ds, qm[jj], NN)
        dqt[jj] += dot(ks, ds, TN)

    def grad_copy(d):
        return pltpu.make_async_remote_copy(
            src_ref=gsend.at[d - 1], dst_ref=grecv.at[d - 1],
            send_sem=g_send.at[d - 1], recv_sem=g_recv.at[d - 1],
            device_id=((sibling, along(-2), along(-1))[d - 1], g), device_id_type=MESH,
        )

    odd_f = odd.astype(F32)

    for d in (3, 1, 2, 0):
        lo = own - d * ROWS
        if d == SPAN:
            for jj in range(PAIRS):
                unit(jj, jj * PAIR, ROWS - jj * PAIR, 0)
        elif d == 0:
            for jj in range(PAIRS):
                unit(jj, lo, (jj + 1) * PAIR, lo - jj * PAIR)
        else:
            def step(jj, carry):
                unit(jj, lo, ROWS, pl.multiple_of(lo - jj * PAIR, PAIR))
                return carry

            lax.fori_loop(0, PAIRS, step, 0)
        dk = dk_acc[lo : lo + ROWS, :] * SCALE
        dv = dv_acc[lo : lo + ROWS, :]
        if d == 2:
            for e in (1, 3):
                arrived(grecv.at[e - 1], g_recv.at[e - 1])
            dk = dk + grecv[2, 0].astype(F32) + odd_f * grecv[0, 0].astype(F32)
            dv = dv + grecv[2, 1].astype(F32) + odd_f * grecv[0, 1].astype(F32)
        if d > 0:
            gsend[d - 1, 0] = dk.astype(BF16)
            gsend[d - 1, 1] = dv.astype(BF16)
            grad_copy(d).start()

    def finish(jj, carry):
        rows = pl.ds(pl.multiple_of(jj * PAIR, PAIR), PAIR)
        dq = (dqt[jj] * (rls[jj] * SCALE)).T
        dq_ref[rows] = dq.reshape(PAIR, QPK, DIM).astype(BF16)
        return carry

    lax.fori_loop(0, PAIRS, finish, 0)

    dk = dk + (1.0 - odd_f) * grecv[0, 0].astype(F32)
    dv = dv + (1.0 - odd_f) * grecv[0, 1].astype(F32)
    arrived(grecv.at[1], g_recv.at[1])
    dk_ref[...] = (dk + grecv[1, 0].astype(F32)).astype(BF16)
    dv_ref[...] = (dv + grecv[1, 1].astype(F32)).astype(BF16)

    for slot, peer in enumerate(peers):
        for i in range(2):
            kv_copy(i, peer, slot).wait_send()
        wide_copy(2, q_ref, qbuf, peer, slot).wait_send()
        wide_copy(3, do_ref, dobuf, peer, slot).wait_send()
    for i in range(2):
        to_two(i).wait_send()
        to_sibling(i, 0).wait_send()
        to_three(i).wait_send()
    for d in range(1, SPAN + 1):
        grad_copy(d).wait_send()


def put_out(*refs):
    sems = refs[-1]
    n = (len(refs) - 1) // 2
    copies = [pltpu.make_async_copy(refs[i], refs[n + i], sems.at[i]) for i in range(n)]
    for copy in copies:
        copy.start()
    for copy in copies:
        copy.wait()


def local(n_ctx, queries, keys, values, grad_out, segment_ids):
    vmem = pl.BlockSpec(memory_space=pltpu.VMEM)
    anywhere = pl.BlockSpec(memory_space=pl.ANY)
    shapes = ((ROWS, QPK, DIM), (ROWS, QPK, DIM), (ROWS, DIM), (ROWS, DIM))
    results = pl.pallas_call(
        functools.partial(kernel, n_ctx),
        out_shape=tuple(pltpu.VMEM(shape, BF16) for shape in shapes),
        in_specs=[anywhere, anywhere, vmem, vmem, vmem],
        out_specs=(vmem,) * 4,
        scratch_shapes=[
            pltpu.VMEM((PIECE * GROUPS, DIM), F32),
            pltpu.VMEM((GROUPS, 2, PIECE, DIM), BF16),
            pltpu.VMEM((2, WINDOW, DIM), BF16),
            pltpu.VMEM((WINDOW, DIM), BF16),
            pltpu.VMEM((ROWS, DIM), F32),
            pltpu.VMEM((ROWS, QPK, DIM), BF16),
            pltpu.VMEM((ROWS, QPK, DIM), BF16),
            pltpu.VMEM((PAIRS, COLS, DIM), BF16),
            pltpu.VMEM((PAIRS, COLS, DIM), BF16),
            pltpu.VMEM((PAIRS, COLS, DIM), BF16),
            pltpu.VMEM((BAND, COLS), F32),
            pltpu.VMEM((PAIRS, BAND, COLS), BF16),
            pltpu.VMEM((PAIRS, 1, COLS), F32),
            pltpu.VMEM((PAIRS, 1, COLS), F32),
            pltpu.VMEM((PAIRS, DIM, COLS), F32),
            pltpu.VMEM((WINDOW, DIM), F32),
            pltpu.VMEM((WINDOW, DIM), F32),
            pltpu.VMEM((SPAN, 2, ROWS, DIM), BF16),
            pltpu.VMEM((SPAN, 2, ROWS, DIM), BF16),
            pltpu.SemaphoreType.DMA((4, GROUPS - 1)),
            pltpu.SemaphoreType.DMA((4, GROUPS)),
            pltpu.SemaphoreType.DMA((2, SPAN)),
            pltpu.SemaphoreType.DMA((2, SPAN)),
            pltpu.SemaphoreType.DMA((SPAN,)),
            pltpu.SemaphoreType.DMA((SPAN,)),
        ],
        compiler_params=pltpu.CompilerParams(
            collective_id=0, has_side_effects=True, vmem_limit_bytes=56 << 20
        ),
        cost_estimate=pl.CostEstimate(
            flops=12 * DIM * PAIRS * BAND * COLS,
            bytes_accessed=4 * 2 * ROWS * QPK * DIM,
            transcendentals=PAIRS * BAND * COLS,
        ),
    )(
        queries.reshape(PIECE, GROUPS, QPK, DIM),
        grad_out.reshape(PIECE, GROUPS, QPK, DIM),
        keys,
        values,
        segment_ids.reshape(-1, DIM),
    )
    attention, grad_queries, grad_keys, grad_values = pl.pallas_call(
        put_out,
        out_shape=tuple(jax.ShapeDtypeStruct(shape, BF16) for shape in shapes),
        in_specs=[vmem] * 4,
        out_specs=(anywhere,) * 4,
        scratch_shapes=[pltpu.SemaphoreType.DMA((4,))],
    )(*results)
    return (
        attention,
        grad_queries,
        grad_keys.reshape(ROWS, 1, DIM),
        grad_values.reshape(ROWS, 1, DIM),
    )


def solution(mesh):
    rows = P(("ctx", "kvh"), None, None)
    heads = P("ctx", "kvh", None)
    return jax.shard_map(
        functools.partial(local, mesh.shape["ctx"]),
        mesh=mesh,
        in_specs=(rows, rows, rows, rows, P()),
        out_specs=(heads, heads, heads, heads),
        check_vma=False,
    )
```

time: 201 us -> 68.3 us (0.34)
  the two profiles are of different devices: /device:TPU:250 before, /device:TPU:64 now
where the time goes in v1:
time: 68.3 us; the launch traced here: 68.2 us
  Pallas kernels  64.5 us (94%)
  local copies, waits for them, and re-layouts  3.05 us (4%)
    pallas_call x1, Pallas kernels, local(): pl.pallas_call(functools.partial(kernel, n_ctx), out_shape=tuple((pltpu.V...  61.8 us
    unnamed x8, local copies, waits for them, and re-layouts  3.05 us
    pallas_call x1, Pallas kernels, local(): pl.pallas_call(put_out, out_shape=tuple((jax.ShapeDtypeStruct(shape, BF16...  2.62 us

profile of v1, /device:TPU:64, one launch (start us, length us, event | category | flops | bytes accessed | tf_op | source)
XLA Modules:
  0.0 68.2 jit_solution(7612881693183605361)
XLA Ops:
  0.6 61.8 %shard_map.84 = (bf16[384,8,128]{2,1,0:T(8,128)(2,1)S(1)}, bf16[384,8,128]{2,1,0:T(8,128)(2,1)S(1)}, bf16[384,128]{1,0:T(8,128)(2,1)S(1)}, bf16[384,128]{1,0:T(8,128)(2,1)S(1)}) custom-call(bf16[48,8,8,128]{3,2,1,0:T(8,128)(2,1)} %bitcast.5, bf16[48,8,8,128]{3,2,1,0:T(8,128)(2,1)} %bitcast.6, bf16[48,8,128]{2,1,0:T(8,128)(2,1)} %k_ref.1, ...), custom_call_target="tpu_custom_call" | custom-call | flops 5888802816 | bytes 3145728 | tf_op jit(solution)/shard_map/pallas_call | solution.py:310
  62.5 0.0 copy-start
  62.5 0.9 %copy-done = bf16[384,8,128]{2,1,0:T(8,128)(2,1)} copy-done((bf16[384,8,128]{2,1,0:T(8,128)(2,1)}, bf16[384,8,128]{2,1,0:T(8,128)(2,1)S(1)}, u32[]{:S(2)}) %copy-start) | copy-done | bytes 786456
  63.4 0.0 copy-start.1
  63.4 0.9 %copy-done.1 = bf16[384,8,128]{2,1,0:T(8,128)(2,1)} copy-done((bf16[384,8,128]{2,1,0:T(8,128)(2,1)}, bf16[384,8,128]{2,1,0:T(8,128)(2,1)S(1)}, u32[]{:S(2)}) %copy-start.1) | copy-done | bytes 786456
  64.3 0.0 copy-start.2
  64.3 0.6 copy-done.2
  64.9 0.0 copy-start.3
  64.9 0.6 copy-done.3
  65.5 2.6 %shard_map.85 = (bf16[384,8,128]{2,1,0:T(8,128)(2,1)}, bf16[384,8,128]{2,1,0:T(8,128)(2,1)}, bf16[384,128]{1,0:T(8,128)(2,1)}, bf16[384,128]{1,0:T(8,128)(2,1)}) custom-call(bf16[384,8,128]{2,1,0:T(8,128)(2,1)} %copy-done, bf16[384,8,128]{2,1,0:T(8,128)(2,1)} %copy-done.1, bf16[384,128]{1,0:T(8,128)(2,1)} %copy-done.2, bf16[384,128]{1,0:T(8,128)(2,1)} %copy-done.3), custom_call_target="tpu_custom_call" | custom-call | tf_op jit(solution)/shard_map/pallas_call | solution.py:357
Async XLA Ops:
  62.5 0.9 %copy-start = (bf16[384,8,128]{2,1,0:T(8,128)(2,1)}, bf16[384,8,128]{2,1,0:T(8,128)(2,1)S(1)}, u32[]{:S(2)}) copy-start(bf16[384,8,128]{2,1,0:T(8,128)(2,1)S(1)} %get-tuple-element.12.refs_0_) | copy-start | bytes 2359300
  63.4 0.9 %copy-start.1 = (bf16[384,8,128]{2,1,0:T(8,128)(2,1)}, bf16[384,8,128]{2,1,0:T(8,128)(2,1)S(1)}, u32[]{:S(2)}) copy-start(bf16[384,8,128]{2,1,0:T(8,128)(2,1)S(1)} %get-tuple-element.13.refs_1_) | copy-start | bytes 2359300
  64.3 0.6 copy-start.2
  64.9 0.6 copy-start.3

commit v2 on v1

--- a/solution.py
+++ b/solution.py
@@ -41,7 +41,7 @@
     q_ref, do_ref, k_ref, v_ref, seg_ref,
     att_ref, dq_ref, dk_ref, dv_ref,
     stage, kvsend, kvwin, ohk, ohq, qbuf, dobuf, qm, dom, doms, s_ref, p_all, delta, rls,
-    dqt, dk_acc, dv_acc, gsend, grecv,
+    rowl, oall, dqt, dk_acc, dv_acc, gsend, grecv,
     a2a_send, a2a_recv, fwd_send, fwd_recv, g_send, g_recv,
 ):
     c = lax.axis_index("ctx")
@@ -103,12 +103,44 @@
         pltpu.make_async_copy(kvsend.at[g, i], kv_slot(i), a2a_recv.at[i, g]).start()
     pltpu.make_async_copy(q_ref.at[:, g], qbuf.at[my_rows], a2a_recv.at[2, g]).start()
     pltpu.make_async_copy(do_ref.at[:, g], dobuf.at[my_rows], a2a_recv.at[3, g]).start()
-    for slot, peer in enumerate(peers):
-        wide_copy(2, q_ref, qbuf, peer, slot).start()
-        wide_copy(3, do_ref, dobuf, peer, slot).start()
+    near = (0, 1, 3)
+    far = (2, 4, 5, 6)
+    for slot in near:
+        wide_copy(2, q_ref, qbuf, peers[slot], slot).start()
 
     def arrived(ref, sem):
         pltpu.make_async_copy(ref, ref, sem).wait()
+
+    def block(i, d):
+        return kvwin.at[i, pl.ds(own - d * ROWS, ROWS)]
+
+    def fwd_copy(i, n, src, d, there):
+        return pltpu.make_async_remote_copy(
+            src_ref=src, dst_ref=block(i, d),
+            send_sem=fwd_send.at[i, n], recv_sem=fwd_recv.at[i, d - 1],
+            device_id=(there, g), device_id_type=MESH,
+        )
+
+    def to_two(i):
+        return fwd_copy(i, 0, block(i, 0), 2, along(2))
+
+    def to_sibling(i, d):
+        return fwd_copy(i, 1, block(i, d), 1, sibling)
+
+    def to_three(i):
+        return fwd_copy(i, 2, block(i, 2), 3, along(1))
+
+    for i in range(2):
+        for j in range(GROUPS):
+            arrived(kvwin.at[i, pl.ds(own + j * PIECE, PIECE)], a2a_recv.at[i, j])
+        to_two(i).start()
+
+        @pl.when(odd == 0)
+        def _():
+            to_sibling(i, 0).start()
+
+    for slot in far:
+        wide_copy(2, q_ref, qbuf, peers[slot], slot).start()
 
     tiles = WINDOW // DIM
     seg_rows = n_ctx * ROWS // DIM
@@ -123,35 +155,6 @@
             ohq[at : at + DIM, :] = (hot - 1.0) * BIG
     dk_acc[...] = jnp.zeros_like(dk_acc)
     dv_acc[...] = jnp.zeros_like(dv_acc)
-    dqt[...] = jnp.zeros_like(dqt)
-
-    def block(i, d):
-        return kvwin.at[i, pl.ds(own - d * ROWS, ROWS)]
-
-    def fwd_copy(i, n, src, d, there):
-        return pltpu.make_async_remote_copy(
-            src_ref=src, dst_ref=block(i, d),
-            send_sem=fwd_send.at[i, n], recv_sem=fwd_recv.at[i, d - 1],
-            device_id=(there, g), device_id_type=MESH,
-        )
-
-    def to_two(i):
-        return fwd_copy(i, 0, block(i, 0), 2, along(2))
-
-    def to_sibling(i, d):
-        return fwd_copy(i, 1, block(i, d), 1, sibling)
-
-    def to_three(i):
-        return fwd_copy(i, 2, block(i, 2), 3, along(1))
-
-    for i in range(2):
-        for j in range(GROUPS):
-            arrived(kvwin.at[i, pl.ds(own + j * PIECE, PIECE)], a2a_recv.at[i, j])
-        to_two(i).start()
-
-        @pl.when(odd == 0)
-        def _():
-            to_sibling(i, 0).start()
 
     for i in range(2):
         arrived(block(i, 2), fwd_recv.at[i, 1])
@@ -161,18 +164,26 @@
         def _():
             to_sibling(i, 2).start()
 
+    for slot, peer in enumerate(peers):
+        wide_copy(3, do_ref, dobuf, peer, slot).start()
+
     for d in (1, 3):
         arrived(block(0, d), fwd_recv.at[0, d - 1])
 
-    def forward(t, carry):
+    def pair(t):
         step = jnp.where(t == 0, 0, jnp.where(t == 1, 3, jnp.where(t == 2, 1, 2)))
         jj = lax.rem(x + step, PAIRS)
-        base = pl.multiple_of(jj * PAIR, PAIR)
-        rows = pl.ds(base, PAIR)
+        return jj, pl.multiple_of(jj * PAIR, PAIR)
+
+    def pair_arrived(i, buf, jj, base):
         for half in range(2):
             piece = pl.ds(pl.multiple_of(base + half * PIECE, PIECE), PIECE)
-            arrived(qbuf.at[piece], a2a_recv.at[2, 2 * jj + half])
-            arrived(dobuf.at[piece], a2a_recv.at[3, 2 * jj + half])
+            arrived(buf.at[piece], a2a_recv.at[i, 2 * jj + half])
+
+    def forward(t, carry):
+        jj, base = pair(t)
+        rows = pl.ds(base, PAIR)
+        pair_arrived(2, qbuf, jj, base)
         qf = qbuf[rows].astype(F32).reshape(COLS, DIM)
         qb = qf.astype(BF16)
         penalty = jnp.broadcast_to(ohq[rows, :][:, None, :], (PAIR, QPK, DIM))
@@ -202,10 +213,8 @@
         rl = 1.0 / jnp.sum(l8, axis=0, keepdims=True)
         rls[jj] = rl
         by_row = jnp.broadcast_to(rl, (DIM, COLS)).T
+        rowl[jj] = by_row
         qm[jj] = (qf * by_row).astype(BF16)
-        dof = dobuf[rows].astype(F32).reshape(COLS, DIM)
-        dom[jj] = dof.astype(BF16)
-        doms[jj] = (dof * by_row).astype(BF16)
 
         @pl.when(t == 0)
         def _():
@@ -215,21 +224,43 @@
         band = pl.ds(base, BAND)
         ot = dot(kvwin[1, band, :], p_all[jj], TN) * rl
         ot = ot.astype(BF16).astype(F32)
+        oall[jj] = ot
         att_ref[rows] = ot.T.reshape(PAIR, QPK, DIM).astype(BF16)
-        delta[jj] = jnp.sum(dof.T * ot, axis=0, keepdims=True)
         return carry
 
     lax.fori_loop(0, PAIRS, forward, 0)
 
-    def unit(jj, key_lo, size, off):
-        keys = slice(key_lo, key_lo + size)
+    def take_grad(jj, base):
+        pair_arrived(3, dobuf, jj, base)
+        dof = dobuf[pl.ds(base, PAIR)].astype(F32).reshape(COLS, DIM)
+        dom[...] = dof.astype(BF16)
+        doms[...] = (dof * rowl[jj]).astype(BF16)
+        delta[...] = jnp.sum(dof.T * oall[jj], axis=0, keepdims=True)
+        dqt[...] = jnp.zeros_like(dqt)
+
+    def unit(jj, keys, size, off):
         ks = kvwin[0, keys, :]
         p = p_all[jj, pl.ds(off, size), :]
-        dpt = dot(kvwin[1, keys, :], dom[jj], NT)
-        ds = p * (dpt - delta[jj]).astype(BF16)
-        dv_acc[keys, :] += dot(p, doms[jj], NN)
+        dpt = dot(kvwin[1, keys, :], dom[...], NT)
+        ds = p * (dpt - delta[...]).astype(BF16)
+        dv_acc[keys, :] += dot(p, doms[...], NN)
         dk_acc[keys, :] += dot(ds, qm[jj], NN)
-        dqt[jj] += dot(ks, ds, TN)
+        dqt[...] += dot(ks, ds, TN)
+
+    def put_dq(jj, base):
+        dq = (dqt[...] * (rls[jj] * SCALE)).T
+        dq_ref[pl.ds(base, PAIR)] = dq.reshape(PAIR, QPK, DIM).astype(BF16)
+
+    def backward(t, carry):
+        jj, base = pair(t)
+        take_grad(jj, base)
+        part = BAND // 3
+        for ch in range(3):
+            unit(jj, pl.ds(pl.multiple_of(base + ch * part, 32), part), part, ch * part)
+        put_dq(jj, base)
+        return carry
+
+    lax.fori_loop(0, PAIRS - 1, backward, 0)
 
     def grad_copy(d):
         return pltpu.make_async_remote_copy(
@@ -240,20 +271,21 @@
 
     odd_f = odd.astype(F32)
 
+    jj, base = pair(PAIRS - 1)
+    take_grad(jj, base)
     for d in (3, 1, 2, 0):
         lo = own - d * ROWS
-        if d == SPAN:
-            for jj in range(PAIRS):
-                unit(jj, jj * PAIR, ROWS - jj * PAIR, 0)
-        elif d == 0:
-            for jj in range(PAIRS):
-                unit(jj, lo, (jj + 1) * PAIR, lo - jj * PAIR)
+        if d in (0, SPAN):
+            for v in range(PAIRS):
+                lo_key = v * PAIR if d else lo
+                size = ROWS - v * PAIR if d else (v + 1) * PAIR
+                off = 0 if d else lo - v * PAIR
+
+                @pl.when(jj == v)
+                def _():
+                    unit(v, pl.ds(lo_key, size), size, off)
         else:
-            def step(jj, carry):
-                unit(jj, lo, ROWS, pl.multiple_of(lo - jj * PAIR, PAIR))
-                return carry
-
-            lax.fori_loop(0, PAIRS, step, 0)
+            unit(jj, pl.ds(lo, ROWS), ROWS, pl.multiple_of(lo - jj * PAIR, PAIR))
         dk = dk_acc[lo : lo + ROWS, :] * SCALE
         dv = dv_acc[lo : lo + ROWS, :]
         if d == 2:
@@ -266,13 +298,7 @@
             gsend[d - 1, 1] = dv.astype(BF16)
             grad_copy(d).start()
 
-    def finish(jj, carry):
-        rows = pl.ds(pl.multiple_of(jj * PAIR, PAIR), PAIR)
-        dq = (dqt[jj] * (rls[jj] * SCALE)).T
-        dq_ref[rows] = dq.reshape(PAIR, QPK, DIM).astype(BF16)
-        return carry
-
-    lax.fori_loop(0, PAIRS, finish, 0)
+    put_dq(jj, base)
 
     dk = dk + (1.0 - odd_f) * grecv[0, 0].astype(F32)
     dv = dv + (1.0 - odd_f) * grecv[0, 1].astype(F32)
@@ -321,13 +347,15 @@
             pltpu.VMEM((ROWS, QPK, DIM), BF16),
             pltpu.VMEM((ROWS, QPK, DIM), BF16),
             pltpu.VMEM((PAIRS, COLS, DIM), BF16),
-            pltpu.VMEM((PAIRS, COLS, DIM), BF16),
-            pltpu.VMEM((PAIRS, COLS, DIM), BF16),
+            pltpu.VMEM((COLS, DIM), BF16),
+            pltpu.VMEM((COLS, DIM), BF16),
             pltpu.VMEM((BAND, COLS), F32),
             pltpu.VMEM((PAIRS, BAND, COLS), BF16),
+            pltpu.VMEM((1, COLS), F32),
             pltpu.VMEM((PAIRS, 1, COLS), F32),
-            pltpu.VMEM((PAIRS, 1, COLS), F32),
+            pltpu.VMEM((PAIRS, COLS, DIM), F32),
             pltpu.VMEM((PAIRS, DIM, COLS), F32),
+            pltpu.VMEM((DIM, COLS), F32),
             pltpu.VMEM((WINDOW, DIM), F32),
             pltpu.VMEM((WINDOW, DIM), F32),
             pltpu.VMEM((SPAN, 2, ROWS, DIM), BF16),
@@ -357,10 +385,11 @@
     attention, grad_queries, grad_keys, grad_values = pl.pallas_call(
         put_out,
         out_shape=tuple(jax.ShapeDtypeStruct(shape, BF16) for shape in shapes),
-        in_specs=[vmem] * 4,
+        in_specs=[anywhere] * 4,
         out_specs=(anywhere,) * 4,
         scratch_shapes=[pltpu.SemaphoreType.DMA((4,))],
-    )(*results)
+        compiler_params=pltpu.CompilerParams(vmem_limit_bytes=1 << 20),
+    )(*[pltpu.with_memory_space_constraint(r, pltpu.VMEM) for r in results])
     return (
         attention,
         grad_queries,

time: 68.3 us -> 62.3 us (0.912)
  local copies, waits for them, and re-layouts: 3.05 us -> 0 us
  Pallas kernels: 64.5 us -> 61.5 us
    unnamed x8 -> x0, local copies, waits for them, and re-layouts: 3.05 us -> none
    pallas_call x1, Pallas kernels: 61.8 us -> 60.2 us  [local(): pl.pallas_call(functools.partial(kernel, n_ctx), out_shape=tuple((pltpu.V...]
    pallas_call x1, Pallas kernels: 2.62 us -> 1.23 us  [local(): pl.pallas_call(put_out, out_shape=tuple((jax.ShapeDtypeStruct(shape, BF16...]
where the time goes in v2:
time: 62.3 us; the launch traced here: 62.1 us
  Pallas kernels  61.5 us (99%)
  between operations  0.64 us (1%)
    pallas_call x1, Pallas kernels, local(): pl.pallas_call(functools.partial(kernel, n_ctx), out_shape=tuple((pltpu.V...  60.2 us

profile of v2, /device:TPU:64, one launch (start us, length us, event | category | flops | bytes accessed | tf_op | source)
XLA Modules:
  0.0 62.1 jit_solution(16020518172551224760)
XLA Ops:
  0.6 60.2 %shard_map.84 = (bf16[384,8,128]{2,1,0:T(8,128)(2,1)S(1)}, bf16[384,8,128]{2,1,0:T(8,128)(2,1)S(1)}, bf16[384,128]{1,0:T(8,128)(2,1)S(1)}, bf16[384,128]{1,0:T(8,128)(2,1)S(1)}) custom-call(bf16[48,8,8,128]{3,2,1,0:T(8,128)(2,1)} %bitcast.5, bf16[48,8,8,128]{3,2,1,0:T(8,128)(2,1)} %bitcast.6, bf16[48,8,128]{2,1,0:T(8,128)(2,1)} %k_ref.1, ...), custom_call_target="tpu_custom_call" | custom-call | flops 5888802816 | bytes 3145728 | tf_op jit(solution)/shard_map/pallas_call | solution.py:336
  60.9 1.2 %shard_map.85 = (bf16[384,8,128]{2,1,0:T(8,128)(2,1)}, bf16[384,8,128]{2,1,0:T(8,128)(2,1)}, bf16[384,128]{1,0:T(8,128)(2,1)}, bf16[384,128]{1,0:T(8,128)(2,1)}) custom-call(bf16[384,8,128]{2,1,0:T(8,128)(2,1)S(1)} %get-tuple-element.12.refs_0_, bf16[384,8,128]{2,1,0:T(8,128)(2,1)S(1)} %get-tuple-element.13.refs_1_, ...), custom_call_target="tpu_custom_call" | custom-call | tf_op jit(solution)/shard_map/pallas_call | solution.py:385

commit v3 on v2

--- a/solution.py
+++ b/solution.py
@@ -10,6 +10,7 @@
 
 MESH = pl.DeviceIdType.MESH
 SPAN = 3
+GROUP = 16
 BIG = 1e30
 F32 = jnp.float32
 BF16 = jnp.bfloat16
@@ -41,8 +42,8 @@
     q_ref, do_ref, k_ref, v_ref, seg_ref,
     att_ref, dq_ref, dk_ref, dv_ref,
     stage, kvsend, kvwin, ohk, ohq, qbuf, dobuf, qm, dom, doms, s_ref, p_all, delta, rls,
-    rowl, oall, dqt, dk_acc, dv_acc, gsend, grecv,
-    a2a_send, a2a_recv, fwd_send, fwd_recv, g_send, g_recv,
+    rowl, oall, dqt, dk_acc, dv_acc, gsend, grecv, rbuf,
+    a2a_send, a2a_recv, rel_send, rel_recv, fwd_send, fwd_recv, g_send, g_recv,
 ):
     c = lax.axis_index("ctx")
     g = lax.axis_index("kvh")
@@ -50,23 +51,50 @@
     odd = lax.rem(c, 2)
     sibling = c + 1 - 2 * odd
 
-    def along(steps):
-        return lax.rem(c + (steps + n_ctx), n_ctx)
-
     barrier = pltpu.get_barrier_semaphore()
     for s in range(1, GROUPS):
         pl.semaphore_signal(
             barrier, inc=1, device_id=(c, lax.rem(g + s, GROUPS)), device_id_type=MESH
         )
-    for steps in (1, -1, 2, -2):
-        pl.semaphore_signal(barrier, inc=1, device_id=(along(steps), g), device_id_type=MESH)
+
+    def before(d):
+        return c >= d
+
+    def behind(d):
+        return c + d < n_ctx
+
+    for d in (1, 2):
+        for there, exists in ((c + d, behind(d)), (c - d, before(d))):
+            @pl.when(exists)
+            def _():
+                pl.semaphore_signal(barrier, inc=1, device_id=(there, g), device_id_type=MESH)
+
+    place = lax.rem(c, GROUP)
+    first_y, last_y = place < 2, place >= GROUP - 2
+    over_on = last_y & behind(2)
+    relay_on = last_y & before(GROUP)
+    greet = (
+        (c + GROUP, over_on),
+        (c - GROUP, relay_on),
+        (c + GROUP - 2, first_y & before(GROUP)),
+        (c - GROUP + 2, relay_on),
+        (c + GROUP - 1, first_y & (odd == 0) & before(GROUP)),
+        (c - GROUP + 1, relay_on & (odd == 1)),
+    )
+    greet = greet if n_ctx > GROUP else ()
+    for there, exists in greet:
+        @pl.when(exists)
+        def _():
+            pl.semaphore_signal(barrier, inc=1, device_id=(there, g), device_id_type=MESH)
 
     for i, ref in enumerate((k_ref, v_ref)):
         stage[...] = ref[...].astype(F32).reshape(PIECE * GROUPS, DIM)
         for h in range(GROUPS):
             kvsend[h, i] = stage[pl.ds(h, PIECE, stride=GROUPS), :].astype(BF16)
 
-    pl.semaphore_wait(barrier, GROUPS - 1 + 4)
+    partners = sum(e(d).astype(jnp.int32) for e in (before, behind) for d in (1, 2))
+    partners = partners + sum(exists.astype(jnp.int32) for _, exists in greet)
+    pl.semaphore_wait(barrier, partners + (GROUPS - 1))
 
     own = SPAN * ROWS
     my_rows = pl.ds(pl.multiple_of(g * PIECE, PIECE), PIECE)
@@ -97,19 +125,22 @@
                 continue
             peers.append(2 * px + lax.rem(z + other, 2))
 
+    wide = ((q_ref, qbuf), (do_ref, dobuf))
+
+    def send_wide(i, slots):
+        for slot in slots:
+            wide_copy(i, *wide[i - 2], peers[slot], slot).start()
+
+    def arrived(ref, sem):
+        pltpu.make_async_copy(ref, ref, sem).wait()
+
     for i in range(2):
         for slot, peer in enumerate(peers):
             kv_copy(i, peer, slot).start()
         pltpu.make_async_copy(kvsend.at[g, i], kv_slot(i), a2a_recv.at[i, g]).start()
+    send_wide(2, (0, 1, 3))
     pltpu.make_async_copy(q_ref.at[:, g], qbuf.at[my_rows], a2a_recv.at[2, g]).start()
     pltpu.make_async_copy(do_ref.at[:, g], dobuf.at[my_rows], a2a_recv.at[3, g]).start()
-    near = (0, 1, 3)
-    far = (2, 4, 5, 6)
-    for slot in near:
-        wide_copy(2, q_ref, qbuf, peers[slot], slot).start()
-
-    def arrived(ref, sem):
-        pltpu.make_async_copy(ref, ref, sem).wait()
 
     def block(i, d):
         return kvwin.at[i, pl.ds(own - d * ROWS, ROWS)]
@@ -122,25 +153,56 @@
         )
 
     def to_two(i):
-        return fwd_copy(i, 0, block(i, 0), 2, along(2))
+        return fwd_copy(i, 0, block(i, 0), 2, c + 2)
 
     def to_sibling(i, d):
         return fwd_copy(i, 1, block(i, d), 1, sibling)
 
     def to_three(i):
-        return fwd_copy(i, 2, block(i, 2), 3, along(1))
+        return fwd_copy(i, 2, block(i, 2), 3, c + 1)
+
+    def to_relay(n):
+        return pltpu.make_async_remote_copy(
+            src_ref=block(0, 2 * n), dst_ref=rbuf.at[n],
+            send_sem=fwd_send.at[0, 2 * n], recv_sem=rel_recv.at[n],
+            device_id=(c + GROUP, g), device_id_type=MESH,
+        )
+
+    def from_relay(n):
+        return pltpu.make_async_remote_copy(
+            src_ref=rbuf.at[n], dst_ref=block(0, 2 + n),
+            send_sem=rel_send.at[n], recv_sem=fwd_recv.at[0, 1 + n],
+            device_id=(c - GROUP + 2 - n, g), device_id_type=MESH,
+        )
+
+    def start_on(i, n, plain, valid):
+        if i == 0 and greet:
+            @pl.when(valid & over_on)
+            def _():
+                to_relay(n).start()
+
+            valid = valid & jnp.logical_not(over_on)
+
+        @pl.when(valid)
+        def _():
+            plain(i).start()
+
+    two = behind(2)
+    three = before(2) & behind(1)
+    even_sibling = odd == 0
+    odd_sibling = (odd == 1) & before(2)
 
     for i in range(2):
         for j in range(GROUPS):
             arrived(kvwin.at[i, pl.ds(own + j * PIECE, PIECE)], a2a_recv.at[i, j])
-        to_two(i).start()
-
-        @pl.when(odd == 0)
+
+        start_on(i, 0, to_two, two)
+
+        @pl.when(even_sibling)
         def _():
             to_sibling(i, 0).start()
 
-    for slot in far:
-        wide_copy(2, q_ref, qbuf, peers[slot], slot).start()
+    send_wide(2, (2, 4, 5, 6))
 
     tiles = WINDOW // DIM
     seg_rows = n_ctx * ROWS // DIM
@@ -156,19 +218,43 @@
     dk_acc[...] = jnp.zeros_like(dk_acc)
     dv_acc[...] = jnp.zeros_like(dv_acc)
 
+    for d in (1, 2, 3):
+        @pl.when(jnp.logical_not(before(d)))
+        def _():
+            kvwin[:, own - d * ROWS : own - (d - 1) * ROWS, :] = jnp.zeros((2, ROWS, DIM), BF16)
+
+    def block_arrived(i, d):
+        @pl.when(before(d))
+        def _():
+            arrived(block(i, d), fwd_recv.at[i, d - 1])
+
     for i in range(2):
-        arrived(block(i, 2), fwd_recv.at[i, 1])
-        to_three(i).start()
-
-        @pl.when(odd == 1)
+        block_arrived(i, 2)
+
+        if i == 0 and greet:
+            start_on(0, 1, to_three, three & (odd == 1))
+
+            @pl.when(three & (odd == 0))
+            def _():
+                to_three(0).start()
+        else:
+            start_on(i, 1, to_three, three)
+
+        @pl.when(odd_sibling)
         def _():
             to_sibling(i, 2).start()
 
-    for slot, peer in enumerate(peers):
-        wide_copy(3, do_ref, dobuf, peer, slot).start()
+    if greet:
+        for n, where in ((0, relay_on), (1, relay_on & (odd == 1))):
+            @pl.when(where)
+            def _():
+                arrived(rbuf.at[n], rel_recv.at[n])
+                from_relay(n).start()
+
+    send_wide(3, range(GROUPS - 1))
 
     for d in (1, 3):
-        arrived(block(0, d), fwd_recv.at[0, d - 1])
+        block_arrived(0, d)
 
     def pair(t):
         step = jnp.where(t == 0, 0, jnp.where(t == 1, 3, jnp.where(t == 2, 1, 2)))
@@ -219,7 +305,7 @@
         @pl.when(t == 0)
         def _():
             for d in (1, 3):
-                arrived(block(1, d), fwd_recv.at[1, d - 1])
+                block_arrived(1, d)
 
         band = pl.ds(base, BAND)
         ot = dot(kvwin[1, band, :], p_all[jj], TN) * rl
@@ -230,93 +316,146 @@
 
     lax.fori_loop(0, PAIRS, forward, 0)
 
-    def take_grad(jj, base):
+    def take_grad(t, carry):
+        jj, base = pair(t)
         pair_arrived(3, dobuf, jj, base)
         dof = dobuf[pl.ds(base, PAIR)].astype(F32).reshape(COLS, DIM)
-        dom[...] = dof.astype(BF16)
-        doms[...] = (dof * rowl[jj]).astype(BF16)
-        delta[...] = jnp.sum(dof.T * oall[jj], axis=0, keepdims=True)
-        dqt[...] = jnp.zeros_like(dqt)
-
-    def unit(jj, keys, size, off):
+        dom[jj] = dof.astype(BF16)
+        doms[jj] = (dof * rowl[jj]).astype(BF16)
+        delta[jj] = jnp.sum(dof.T * oall[jj], axis=0, keepdims=True)
+        return carry
+
+    lax.fori_loop(0, PAIRS, take_grad, 0)
+
+    def unit(jj, lo, size, off, first=False):
+        keys = pl.ds(lo, size)
         ks = kvwin[0, keys, :]
         p = p_all[jj, pl.ds(off, size), :]
-        dpt = dot(kvwin[1, keys, :], dom[...], NT)
-        ds = p * (dpt - delta[...]).astype(BF16)
-        dv_acc[keys, :] += dot(p, doms[...], NN)
+        dpt = dot(kvwin[1, keys, :], dom[jj], NT)
+        ds = p * (dpt - delta[jj]).astype(BF16)
+        dv_acc[keys, :] += dot(p, doms[jj], NN)
         dk_acc[keys, :] += dot(ds, qm[jj], NN)
-        dqt[...] += dot(ks, ds, TN)
-
-    def put_dq(jj, base):
-        dq = (dqt[...] * (rls[jj] * SCALE)).T
-        dq_ref[pl.ds(base, PAIR)] = dq.reshape(PAIR, QPK, DIM).astype(BF16)
-
-    def backward(t, carry):
-        jj, base = pair(t)
-        take_grad(jj, base)
-        part = BAND // 3
-        for ch in range(3):
-            unit(jj, pl.ds(pl.multiple_of(base + ch * part, 32), part), part, ch * part)
-        put_dq(jj, base)
+        if first:
+            dqt[jj] = dot(ks, ds, TN)
+        else:
+            dqt[jj] += dot(ks, ds, TN)
+
+    def put_dq(jj, carry):
+        dq = (dqt[jj] * (rls[jj] * SCALE)).T
+        rows = pl.ds(pl.multiple_of(jj * PAIR, PAIR), PAIR)
+        dq_ref[rows] = dq.reshape(PAIR, QPK, DIM).astype(BF16)
         return carry
-
-    lax.fori_loop(0, PAIRS - 1, backward, 0)
 
     def grad_copy(d):
         return pltpu.make_async_remote_copy(
             src_ref=gsend.at[d - 1], dst_ref=grecv.at[d - 1],
             send_sem=g_send.at[d - 1], recv_sem=g_recv.at[d - 1],
-            device_id=((sibling, along(-2), along(-1))[d - 1], g), device_id_type=MESH,
+            device_id=((sibling, c - 2, c - 1)[d - 1], g), device_id_type=MESH,
         )
 
     odd_f = odd.astype(F32)
-
-    jj, base = pair(PAIRS - 1)
-    take_grad(jj, base)
-    for d in (3, 1, 2, 0):
-        lo = own - d * ROWS
-        if d in (0, SPAN):
-            for v in range(PAIRS):
-                lo_key = v * PAIR if d else lo
-                size = ROWS - v * PAIR if d else (v + 1) * PAIR
-                off = 0 if d else lo - v * PAIR
-
-                @pl.when(jj == v)
-                def _():
-                    unit(v, pl.ds(lo_key, size), size, off)
-        else:
-            unit(jj, pl.ds(lo, ROWS), ROWS, pl.multiple_of(lo - jj * PAIR, PAIR))
-        dk = dk_acc[lo : lo + ROWS, :] * SCALE
-        dv = dv_acc[lo : lo + ROWS, :]
+    sends = ((odd == 1) | before(2), before(2), before(3))
+    takes = ((odd == 0) | before(3), behind(2), behind(1) & before(2))
+
+    def grad_arrived(d):
+        @pl.when(takes[d - 1])
+        def _():
+            arrived(grecv.at[d - 1], g_recv.at[d - 1])
+
+        @pl.when(jnp.logical_not(takes[d - 1]))
+        def _():
+            grecv[d - 1] = jnp.zeros((2, ROWS, DIM), BF16)
+
+    def terms(d):
+        rows = slice(own - d * ROWS, own - d * ROWS + ROWS)
+        return dk_acc[rows, :] * SCALE, dv_acc[rows, :]
+
+    def send_terms(d, with_sibling=False):
+        dk, dv = terms(d)
         if d == 2:
-            for e in (1, 3):
-                arrived(grecv.at[e - 1], g_recv.at[e - 1])
-            dk = dk + grecv[2, 0].astype(F32) + odd_f * grecv[0, 0].astype(F32)
-            dv = dv + grecv[2, 1].astype(F32) + odd_f * grecv[0, 1].astype(F32)
-        if d > 0:
-            gsend[d - 1, 0] = dk.astype(BF16)
-            gsend[d - 1, 1] = dv.astype(BF16)
+            grad_arrived(3)
+            dk = dk + grecv[2, 0].astype(F32)
+            dv = dv + grecv[2, 1].astype(F32)
+        if with_sibling:
+            dk = dk + grecv[0, 0].astype(F32)
+            dv = dv + grecv[0, 1].astype(F32)
+        gsend[d - 1, 0] = dk.astype(BF16)
+        gsend[d - 1, 1] = dv.astype(BF16)
+
+        @pl.when(sends[d - 1])
+        def _():
             grad_copy(d).start()
 
-    put_dq(jj, base)
+    def whole_block(d):
+        lo = pl.multiple_of(own - d * ROWS, ROWS)
+
+        def step(jj, carry):
+            unit(jj, lo, ROWS, pl.multiple_of(lo - jj * PAIR, PAIR))
+            return carry
+
+        lax.fori_loop(0, PAIRS, step, 0)
+
+    for jj in range(PAIRS):
+        unit(jj, jj * PAIR, ROWS - jj * PAIR, 0, first=True)
+    send_terms(3)
+    whole_block(1 + odd)
+
+    @pl.when(odd == 0)
+    def _():
+        send_terms(1)
+
+    @pl.when(odd == 1)
+    def _():
+        grad_arrived(1)
+        send_terms(2, with_sibling=True)
+
+    whole_block(2 - odd)
+
+    @pl.when(odd == 0)
+    def _():
+        send_terms(2)
+
+    @pl.when(odd == 1)
+    def _():
+        send_terms(1)
+
+    for jj in range(PAIRS):
+        unit(jj, own, (jj + 1) * PAIR, own - jj * PAIR)
+
+    lax.fori_loop(0, PAIRS, put_dq, 0)
+
+    dk, dv = terms(0)
+
+    @pl.when(odd == 0)
+    def _():
+        grad_arrived(1)
 
     dk = dk + (1.0 - odd_f) * grecv[0, 0].astype(F32)
     dv = dv + (1.0 - odd_f) * grecv[0, 1].astype(F32)
-    arrived(grecv.at[1], g_recv.at[1])
+    grad_arrived(2)
     dk_ref[...] = (dk + grecv[1, 0].astype(F32)).astype(BF16)
     dv_ref[...] = (dv + grecv[1, 1].astype(F32)).astype(BF16)
 
     for slot, peer in enumerate(peers):
         for i in range(2):
             kv_copy(i, peer, slot).wait_send()
-        wide_copy(2, q_ref, qbuf, peer, slot).wait_send()
-        wide_copy(3, do_ref, dobuf, peer, slot).wait_send()
+            wide_copy(2 + i, *wide[i], peer, slot).wait_send()
     for i in range(2):
-        to_two(i).wait_send()
-        to_sibling(i, 0).wait_send()
-        to_three(i).wait_send()
+        for copy, sent in (
+            (to_two(i), two), (to_sibling(i, 0), even_sibling | odd_sibling), (to_three(i), three)
+        ):
+            @pl.when(sent)
+            def _():
+                copy.wait_send()
     for d in range(1, SPAN + 1):
-        grad_copy(d).wait_send()
+        @pl.when(sends[d - 1])
+        def _():
+            grad_copy(d).wait_send()
+    if greet:
+        for n, where in ((0, relay_on), (1, relay_on & (odd == 1))):
+            @pl.when(where)
+            def _():
+                from_relay(n).wait_send()
 
 
 def put_out(*refs):
@@ -347,21 +486,24 @@
             pltpu.VMEM((ROWS, QPK, DIM), BF16),
             pltpu.VMEM((ROWS, QPK, DIM), BF16),
             pltpu.VMEM((PAIRS, COLS, DIM), BF16),
-            pltpu.VMEM((COLS, DIM), BF16),
-            pltpu.VMEM((COLS, DIM), BF16),
+            pltpu.VMEM((PAIRS, COLS, DIM), BF16),
+            pltpu.VMEM((PAIRS, COLS, DIM), BF16),
             pltpu.VMEM((BAND, COLS), F32),
             pltpu.VMEM((PAIRS, BAND, COLS), BF16),
-            pltpu.VMEM((1, COLS), F32),
+            pltpu.VMEM((PAIRS, 1, COLS), F32),
             pltpu.VMEM((PAIRS, 1, COLS), F32),
             pltpu.VMEM((PAIRS, COLS, DIM), F32),
             pltpu.VMEM((PAIRS, DIM, COLS), F32),
-            pltpu.VMEM((DIM, COLS), F32),
+            pltpu.VMEM((PAIRS, DIM, COLS), F32),
             pltpu.VMEM((WINDOW, DIM), F32),
             pltpu.VMEM((WINDOW, DIM), F32),
             pltpu.VMEM((SPAN, 2, ROWS, DIM), BF16),
             pltpu.VMEM((SPAN, 2, ROWS, DIM), BF16),
+            pltpu.VMEM((2, ROWS, DIM), BF16),
             pltpu.SemaphoreType.DMA((4, GROUPS - 1)),
             pltpu.SemaphoreType.DMA((4, GROUPS)),
+            pltpu.SemaphoreType.DMA((2,)),
+            pltpu.SemaphoreType.DMA((2,)),
             pltpu.SemaphoreType.DMA((2, SPAN)),
             pltpu.SemaphoreType.DMA((2, SPAN)),
             pltpu.SemaphoreType.DMA((SPAN,)),

time: 62.3 us -> 59.2 us (0.950)
  the two profiles are of different devices: /device:TPU:64 before, /device:TPU:184 now
where the time goes in v3:
time: 59.2 us; the launch traced here: 59.1 us
  Pallas kernels  58.5 us (99%)
  between operations  0.64 us (1%)
    pallas_call x1, Pallas kernels, local(): pl.pallas_call(functools.partial(kernel, n_ctx), out_shape=tuple((pltpu.V...  57.2 us
    pallas_call x1, Pallas kernels, local(): pl.pallas_call(put_out, out_shape=tuple((jax.ShapeDtypeStruct(shape, BF16...  1.23 us

profile of v3, /device:TPU:184, one launch (start us, length us, event | category | flops | bytes accessed | tf_op | source)
XLA Modules:
  0.0 59.1 jit_solution(7462056968729967098)
XLA Ops:
  0.6 57.2 %shard_map.84 = (bf16[384,8,128]{2,1,0:T(8,128)(2,1)S(1)}, bf16[384,8,128]{2,1,0:T(8,128)(2,1)S(1)}, bf16[384,128]{1,0:T(8,128)(2,1)S(1)}, bf16[384,128]{1,0:T(8,128)(2,1)S(1)}) custom-call(bf16[48,8,8,128]{3,2,1,0:T(8,128)(2,1)} %bitcast.5, bf16[48,8,8,128]{3,2,1,0:T(8,128)(2,1)} %bitcast.6, bf16[48,8,128]{2,1,0:T(8,128)(2,1)} %k_ref.1, ...), custom_call_target="tpu_custom_call" | custom-call | flops 5888802816 | bytes 3145728 | tf_op jit(solution)/shard_map/pallas_call | solution.py:475
  57.9 1.2 %shard_map.85 = (bf16[384,8,128]{2,1,0:T(8,128)(2,1)}, bf16[384,8,128]{2,1,0:T(8,128)(2,1)}, bf16[384,128]{1,0:T(8,128)(2,1)}, bf16[384,128]{1,0:T(8,128)(2,1)}) custom-call(bf16[384,8,128]{2,1,0:T(8,128)(2,1)S(1)} %get-tuple-element.12.refs_0_, bf16[384,8,128]{2,1,0:T(8,128)(2,1)S(1)} %get-tuple-element.13.refs_1_, ...), custom_call_target="tpu_custom_call" | custom-call | tf_op jit(solution)/shard_map/pallas_call | solution.py:527

commit v4 on v3

--- a/solution.py
+++ b/solution.py
@@ -266,55 +266,80 @@
             piece = pl.ds(pl.multiple_of(base + half * PIECE, PIECE), PIECE)
             arrived(buf.at[piece], a2a_recv.at[i, 2 * jj + half])
 
-    def forward(t, carry):
+    part = BAND // 3
+
+    def load_pair(t):
         jj, base = pair(t)
         rows = pl.ds(base, PAIR)
         pair_arrived(2, qbuf, jj, base)
         qf = qbuf[rows].astype(F32).reshape(COLS, DIM)
-        qb = qf.astype(BF16)
         penalty = jnp.broadcast_to(ohq[rows, :][:, None, :], (PAIR, QPK, DIM))
-        qa = jnp.concatenate([qb, penalty.reshape(COLS, DIM).astype(BF16)], axis=1)
-        part = BAND // 3
-        m8 = None
-        for ch in range(3):
-            keys = pl.ds(pl.multiple_of(base + ch * part, 32), part)
-            ka = jnp.concatenate([kvwin[0, keys, :], ohk[keys, :]], axis=1)
-            s = dot(ka, qa, NT)
-            if ch == 2:
-                tail = s[part - PAIR :]
-                key_at = lax.broadcasted_iota(jnp.int32, (PAIR, COLS), 0) * QPK
-                col_at = lax.broadcasted_iota(jnp.int32, (PAIR, COLS), 1)
-                tail = jnp.where(key_at <= col_at, tail, -BIG)
-                s = jnp.concatenate([s[: part - PAIR], tail], axis=0)
-            s_ref[ch * part : (ch + 1) * part, :] = s
-            top = jnp.max(s.reshape(part // 8, 8, COLS), axis=0)
-            m8 = top if m8 is None else jnp.maximum(m8, top)
-        m = jnp.max(m8, axis=0, keepdims=True)
-        l8 = jnp.zeros((8, COLS), F32)
-        for ch in range(BAND // PAIR):
+        penalty = penalty.reshape(COLS, DIM).astype(BF16)
+        return jj, base, qf, jnp.concatenate([qf.astype(BF16), penalty], axis=1)
+
+    def scores(work, buf, ch):
+        _, base, _, qa = work
+        keys = pl.ds(pl.multiple_of(base + ch * part, 32), part)
+        ka = jnp.concatenate([kvwin[0, keys, :], ohk[keys, :]], axis=1)
+        s = dot(ka, qa, NT)
+        if ch == 2:
+            tail = s[part - PAIR :]
+            key_at = lax.broadcasted_iota(jnp.int32, (PAIR, COLS), 0) * QPK
+            col_at = lax.broadcasted_iota(jnp.int32, (PAIR, COLS), 1)
+            tail = jnp.where(key_at <= col_at, tail, -BIG)
+            s = jnp.concatenate([s[: part - PAIR], tail], axis=0)
+        s_ref[buf, ch * part : (ch + 1) * part, :] = s
+        return jnp.max(s.reshape(part // 8, 8, COLS), axis=0)
+
+    def top(parts):
+        return jnp.max(functools.reduce(jnp.maximum, parts), axis=0, keepdims=True)
+
+    def exponentials(work, buf, m, chunks):
+        total = jnp.zeros((8, COLS), F32)
+        for ch in chunks:
             at = slice(ch * PAIR, (ch + 1) * PAIR)
-            e = jnp.exp2((s_ref[at, :] - m) * (SCALE * LOG2E))
-            l8 = l8 + jnp.sum(e.reshape(PAIR // 8, 8, COLS), axis=0)
-            p_all[jj, at, :] = e.astype(BF16)
-        rl = 1.0 / jnp.sum(l8, axis=0, keepdims=True)
+            e = jnp.exp2((s_ref[buf, at, :] - m) * (SCALE * LOG2E))
+            total = total + jnp.sum(e.reshape(PAIR // 8, 8, COLS), axis=0)
+            p_all[work[0], at, :] = e.astype(BF16)
+        return total
+
+    def weigh(work, total):
+        jj, _, qf, _ = work
+        rl = 1.0 / jnp.sum(total, axis=0, keepdims=True)
         rls[jj] = rl
         by_row = jnp.broadcast_to(rl, (DIM, COLS)).T
         rowl[jj] = by_row
         qm[jj] = (qf * by_row).astype(BF16)
-
-        @pl.when(t == 0)
+        return rl
+
+    def attend(work, rl):
+        jj, base, _, _ = work
+        ot = dot(kvwin[1, pl.ds(base, BAND), :], p_all[jj], TN) * rl
+        ot = ot.astype(BF16).astype(F32)
+        oall[jj] = ot
+        att_ref[pl.ds(base, PAIR)] = ot.T.reshape(PAIR, QPK, DIM).astype(BF16)
+
+    def forward(h, carry):
+        one, two_ = load_pair(2 * h), load_pair(2 * h + 1)
+        m_one = top([scores(one, 0, ch) for ch in range(3)])
+
+        @pl.when(h == 0)
         def _():
             for d in (1, 3):
                 block_arrived(1, d)
 
-        band = pl.ds(base, BAND)
-        ot = dot(kvwin[1, band, :], p_all[jj], TN) * rl
-        ot = ot.astype(BF16).astype(F32)
-        oall[jj] = ot
-        att_ref[rows] = ot.T.reshape(PAIR, QPK, DIM).astype(BF16)
+        tops, total = [], 0.0
+        for ch, chunks in enumerate((range(5), range(5, 9), range(9, 13))):
+            tops.append(scores(two_, 1, ch))
+            total = total + exponentials(one, 0, m_one, chunks)
+        rl_one = weigh(one, total)
+        m_two = top(tops)
+        attend(one, rl_one)
+        total = exponentials(two_, 1, m_two, range(13))
+        attend(two_, weigh(two_, total))
         return carry
 
-    lax.fori_loop(0, PAIRS, forward, 0)
+    lax.fori_loop(0, PAIRS // 2, forward, 0)
 
     def take_grad(t, carry):
         jj, base = pair(t)
@@ -488,7 +513,7 @@
             pltpu.VMEM((PAIRS, COLS, DIM), BF16),
             pltpu.VMEM((PAIRS, COLS, DIM), BF16),
             pltpu.VMEM((PAIRS, COLS, DIM), BF16),
-            pltpu.VMEM((BAND, COLS), F32),
+            pltpu.VMEM((2, BAND, COLS), F32),
             pltpu.VMEM((PAIRS, BAND, COLS), BF16),
             pltpu.VMEM((PAIRS, 1, COLS), F32),
             pltpu.VMEM((PAIRS, 1, COLS), F32),

time: 59.2 us -> 58.6 us (0.990)
  Pallas kernels: 58.5 us -> 57.8 us
    pallas_call x1, Pallas kernels: 57.2 us -> 56.5 us  [local(): pl.pallas_call(functools.partial(kernel, n_ctx), out_shape=tuple((pltpu.V...]
where the time goes in v4:
time: 58.6 us; the launch traced here: 58.4 us
  Pallas kernels  57.8 us (99%)
  between operations  0.64 us (1%)
    pallas_call x1, Pallas kernels, local(): pl.pallas_call(functools.partial(kernel, n_ctx), out_shape=tuple((pltpu.V...  56.5 us
    pallas_call x1, Pallas kernels, local(): pl.pallas_call(put_out, out_shape=tuple((jax.ShapeDtypeStruct(shape, BF16...  1.23 us

profile of v4, /device:TPU:184, one launch (start us, length us, event | category | flops | bytes accessed | tf_op | source)
XLA Modules:
  0.0 58.4 jit_solution(9068680519057143115)
XLA Ops:
  0.6 56.5 %shard_map.84 = (bf16[384,8,128]{2,1,0:T(8,128)(2,1)S(1)}, bf16[384,8,128]{2,1,0:T(8,128)(2,1)S(1)}, bf16[384,128]{1,0:T(8,128)(2,1)S(1)}, bf16[384,128]{1,0:T(8,128)(2,1)S(1)}) custom-call(bf16[48,8,8,128]{3,2,1,0:T(8,128)(2,1)} %bitcast.5, bf16[48,8,8,128]{3,2,1,0:T(8,128)(2,1)} %bitcast.6, bf16[48,8,128]{2,1,0:T(8,128)(2,1)} %k_ref.1, ...), custom_call_target="tpu_custom_call" | custom-call | flops 5888802816 | bytes 3145728 | tf_op jit(solution)/shard_map/pallas_call | solution.py:500
  57.2 1.2 %shard_map.85 = (bf16[384,8,128]{2,1,0:T(8,128)(2,1)}, bf16[384,8,128]{2,1,0:T(8,128)(2,1)}, bf16[384,128]{1,0:T(8,128)(2,1)}, bf16[384,128]{1,0:T(8,128)(2,1)}) custom-call(bf16[384,8,128]{2,1,0:T(8,128)(2,1)S(1)} %get-tuple-element.12.refs_0_, bf16[384,8,128]{2,1,0:T(8,128)(2,1)S(1)} %get-tuple-element.13.refs_1_, ...), custom_call_target="tpu_custom_call" | custom-call | tf_op jit(solution)/shard_map/pallas_call | solution.py:552

commit v5 on v4

--- a/solution.py
+++ b/solution.py
@@ -348,11 +348,10 @@
         dom[jj] = dof.astype(BF16)
         doms[jj] = (dof * rowl[jj]).astype(BF16)
         delta[jj] = jnp.sum(dof.T * oall[jj], axis=0, keepdims=True)
+        dqt[jj] = jnp.zeros((DIM, COLS), F32)
         return carry
 
-    lax.fori_loop(0, PAIRS, take_grad, 0)
-
-    def unit(jj, lo, size, off, first=False):
+    def unit(jj, lo, size, off):
         keys = pl.ds(lo, size)
         ks = kvwin[0, keys, :]
         p = p_all[jj, pl.ds(off, size), :]
@@ -360,16 +359,26 @@
         ds = p * (dpt - delta[jj]).astype(BF16)
         dv_acc[keys, :] += dot(p, doms[jj], NN)
         dk_acc[keys, :] += dot(ds, qm[jj], NN)
-        if first:
-            dqt[jj] = dot(ks, ds, TN)
-        else:
-            dqt[jj] += dot(ks, ds, TN)
-
-    def put_dq(jj, carry):
+        dqt[jj] += dot(ks, ds, TN)
+
+    def put_dq(t, carry):
+        jj, _ = pair(t)
         dq = (dqt[jj] * (rls[jj] * SCALE)).T
         rows = pl.ds(pl.multiple_of(jj * PAIR, PAIR), PAIR)
         dq_ref[rows] = dq.reshape(PAIR, QPK, DIM).astype(BF16)
         return carry
+
+    early = PAIRS // 2
+
+    def backward(t, carry):
+        take_grad(t, 0)
+        jj, base = pair(t)
+        for ch in range(3):
+            unit(jj, pl.multiple_of(base + ch * part, 32), part, ch * part)
+        return put_dq(t, carry)
+
+    lax.fori_loop(0, early, backward, 0)
+    lax.fori_loop(early, PAIRS, take_grad, 0)
 
     def grad_copy(d):
         return pltpu.make_async_remote_copy(
@@ -414,14 +423,28 @@
     def whole_block(d):
         lo = pl.multiple_of(own - d * ROWS, ROWS)
 
-        def step(jj, carry):
+        def step(t, carry):
+            jj, _ = pair(t)
             unit(jj, lo, ROWS, pl.multiple_of(lo - jj * PAIR, PAIR))
             return carry
 
-        lax.fori_loop(0, PAIRS, step, 0)
-
-    for jj in range(PAIRS):
-        unit(jj, jj * PAIR, ROWS - jj * PAIR, 0, first=True)
+        lax.fori_loop(early, PAIRS, step, 0)
+
+    def end_block(far):
+        def step(t, carry):
+            jj, _ = pair(t)
+            for v in range(PAIRS):
+                @pl.when(jj == v)
+                def _():
+                    if far:
+                        unit(v, v * PAIR, ROWS - v * PAIR, 0)
+                    else:
+                        unit(v, own, (v + 1) * PAIR, own - v * PAIR)
+            return carry
+
+        lax.fori_loop(early, PAIRS, step, 0)
+
+    end_block(True)
     send_terms(3)
     whole_block(1 + odd)
 
@@ -444,10 +467,8 @@
     def _():
         send_terms(1)
 
-    for jj in range(PAIRS):
-        unit(jj, own, (jj + 1) * PAIR, own - jj * PAIR)
-
-    lax.fori_loop(0, PAIRS, put_dq, 0)
+    end_block(False)
+    lax.fori_loop(early, PAIRS, put_dq, 0)
 
     dk, dv = terms(0)
 

time: 58.6 us -> 60 us (1.024)
  Pallas kernels: 57.8 us -> 59 us
    pallas_call x1, Pallas kernels: 56.5 us -> 57.8 us  [local(): pl.pallas_call(functools.partial(kernel, n_ctx), out_shape=tuple((pltpu.V...]
where the time goes in v5:
time: 60 us; the launch traced here: 59.8 us
  Pallas kernels  59 us (98%)
  between operations  0.8 us (1%)
    pallas_call x1, Pallas kernels, local(): pl.pallas_call(functools.partial(kernel, n_ctx), out_shape=tuple((pltpu.V...  57.8 us
    pallas_call x1, Pallas kernels, local(): pl.pallas_call(put_out, out_shape=tuple((jax.ShapeDtypeStruct(shape, BF16...  1.23 us

profile of v5, /device:TPU:184, one launch (start us, length us, event | category | flops | bytes accessed | tf_op | source)
XLA Modules:
  0.0 59.8 jit_solution(9422959605403872275)
XLA Ops:
  0.6 57.8 %shard_map.84 = (bf16[384,8,128]{2,1,0:T(8,128)(2,1)S(1)}, bf16[384,8,128]{2,1,0:T(8,128)(2,1)S(1)}, bf16[384,128]{1,0:T(8,128)(2,1)S(1)}, bf16[384,128]{1,0:T(8,128)(2,1)S(1)}) custom-call(bf16[48,8,8,128]{3,2,1,0:T(8,128)(2,1)} %bitcast.5, bf16[48,8,8,128]{3,2,1,0:T(8,128)(2,1)} %bitcast.6, bf16[48,8,128]{2,1,0:T(8,128)(2,1)} %k_ref.1, ...), custom_call_target="tpu_custom_call" | custom-call | flops 5888802816 | bytes 3145728 | tf_op jit(solution)/shard_map/pallas_call | solution.py:521
  58.4 1.2 %shard_map.85 = (bf16[384,8,128]{2,1,0:T(8,128)(2,1)}, bf16[384,8,128]{2,1,0:T(8,128)(2,1)}, bf16[384,128]{1,0:T(8,128)(2,1)}, bf16[384,128]{1,0:T(8,128)(2,1)}) custom-call(bf16[384,8,128]{2,1,0:T(8,128)(2,1)S(1)} %get-tuple-element.12.refs_0_, bf16[384,8,128]{2,1,0:T(8,128)(2,1)S(1)} %get-tuple-element.13.refs_1_, ...), custom_call_target="tpu_custom_call" | custom-call | tf_op jit(solution)/shard_map/pallas_call | solution.py:573
